TPU v7x, 32 devices: a whole 2x2x4 slice. The times are simulated.
32 devices in a mesh: grp: 4 (over x, core), sub: 8 (over z, y).
Axes of the slice: x: 2, y: 2, z: 4, core: 2. Of those that a mesh axis runs over, the one named last changes fastest.
Arguments:
- template: bfloat16 [96, 96, 128], P('sub'), may hold values from -4 to 4
- subjects: bfloat16 [32, 96, 96, 128], P(('grp', 'sub')), may hold values from -40 to 40
Outputs:
- velocity: float32 [96, 3, 96, 128], P('sub')
- new_template: float32 [96, 96, 128], P('sub')
- similarity: float32 [], replicated
All inputs are finite; a program needn't handle non-finite values.
Results may differ from a plain program's by a relative error of at most 0.0003.
Values may be sent and summed in bfloat16 or wider, within the bound.
A program may use at most 128 MiB of HBM per device.

v0:
```python
import math

import jax
import jax.numpy as jnp
from jax import lax
from jax.sharding import PartitionSpec as P

RADIUS = 4
REACH = 5


EPSILON = 1e-05
STEP_LENGTH = 0.5
VARIANCE = 3.0
HIGH = lax.Precision.HIGHEST


def padded_2(x, sides, width):
    for axis, dim in sides:
        devices, length = (lax.axis_size(axis), x.shape[dim])
        up = [(i, (i + 1) % devices) for i in range(devices - 1)]
        down = [(j, i) for i, j in up]
        last = lax.slice_in_dim(x, length - width, length, axis=dim)
        initial = lax.slice_in_dim(x, 0, width, axis=dim)
        before = lax.ppermute(last, axis, up)
        after = lax.ppermute(initial, axis, down)
        x = jnp.concatenate([before, x, after], axis=dim)
    return x


def band_matrix(length, extent, weighted):
    row_ids = lax.broadcasted_iota(jnp.int32, (length, length), 0)
    col_ids = lax.broadcasted_iota(jnp.int32, (length, length), 1)
    inside = jnp.abs(row_ids - col_ids) <= extent
    if weighted:
        kernel_sum = sum(
            (math.exp(-offset * offset / (2.0 * VARIANCE)) for offset in range(-extent, extent + 1))
        )
        offset_f = (row_ids - col_ids).astype(jnp.float32)
        values = jnp.exp(-offset_f * offset_f / (2.0 * VARIANCE)) / kernel_sum
        return jnp.where(inside, values, 0.0)
    return jnp.where(inside, 1.0 / (2 * extent + 1), 0.0).astype(jnp.float32)


def filter_volume(volume, along_z, along_x, along_y):
    result = jnp.dot(volume, along_y, precision=HIGH, preferred_element_type=jnp.float32)
    result = jnp.einsum(
        "ab,zby->zay", along_x, result, precision=HIGH, preferred_element_type=jnp.float32
    )
    return jnp.einsum(
        "ab,bxy->axy", along_z, result, precision=HIGH, preferred_element_type=jnp.float32
    )


def central(volume):
    padded = jnp.pad(volume, 1)
    along_z = (padded[2:, 1:-1, 1:-1] - padded[:-2, 1:-1, 1:-1]) * 0.5
    along_x = (padded[1:-1, 2:, 1:-1] - padded[1:-1, :-2, 1:-1]) * 0.5
    along_y = (padded[1:-1, 1:-1, 2:] - padded[1:-1, 1:-1, :-2]) * 0.5
    return jnp.stack([along_z, along_x, along_y], axis=1)


def on_device(template, subjects):
    fixed_image = lax.all_gather(template, "sub", axis=0, tiled=True).astype(jnp.float32)
    depth, height, width = fixed_image.shape
    box_z = band_matrix(depth, RADIUS, False)
    box_x = band_matrix(height, RADIUS, False)
    box_y = band_matrix(width, RADIUS, False)
    gauss_z = band_matrix(depth, REACH, True)
    gauss_x = band_matrix(height, REACH, True)
    gauss_y = band_matrix(width, REACH, True)
    mean_i = filter_volume(fixed_image, box_z, box_x, box_y)
    mean_ii = filter_volume(fixed_image * fixed_image, box_z, box_x, box_y)
    var_i = mean_ii - mean_i * mean_i
    centred_i = fixed_image - mean_i
    gradients = central(fixed_image)
    moving = subjects[0].astype(jnp.float32)
    mean_j = filter_volume(moving, box_z, box_x, box_y)
    mean_jj = filter_volume(moving * moving, box_z, box_x, box_y)
    mean_ij = filter_volume(fixed_image * moving, box_z, box_x, box_y)
    cross_sum = mean_ij - mean_i * mean_j
    var_j = mean_jj - mean_j * mean_j
    denominator = var_i * var_j + EPSILON
    factor = (
        2.0
        * cross_sum
        / denominator
        * (moving - mean_j - cross_sum / (var_i + EPSILON) * centred_i)
    )
    force_total = factor[:, None] * gradients
    cc_local = jnp.sum(cross_sum * cross_sum / denominator)
    planar = jnp.einsum(
        "zcxb,ba->zcxa", force_total, gauss_y, precision=HIGH, preferred_element_type=jnp.float32
    )
    planar = jnp.einsum(
        "ab,zcby->zcay", gauss_x, planar, precision=HIGH, preferred_element_type=jnp.float32
    )
    group_count = lax.axis_size("grp")
    subject_count = subjects.shape[0] * group_count * lax.axis_size("sub")
    smooth = jnp.einsum(
        "ab,bcxy->acxy", gauss_z, planar, precision=HIGH, preferred_element_type=jnp.float32
    )
    stacked = jnp.concatenate([smooth, moving[:, None]], axis=1)
    group_part = lax.psum_scatter(stacked, "grp", scatter_dimension=2, tiled=True)
    owner_part = lax.psum_scatter(group_part, "sub", scatter_dimension=0, tiled=True)
    summed = lax.all_gather(owner_part, "grp", axis=2, tiled=True)
    mean_velocity = summed[:, :3] / subject_count
    mean_image = summed[:, 3] / subject_count
    padded_mean = padded_2(mean_image, (("sub", 0),), 1)
    velocity_square = jnp.sum(mean_velocity * mean_velocity)
    image_square = jnp.sum(mean_image * mean_image)
    cc_total = lax.psum(cc_local, ("grp", "sub"))
    velocity_total, image_sq_total = lax.psum((velocity_square, image_square), "sub")
    cell_count = depth * height * width
    velocity_norm = jnp.sqrt(velocity_total / cell_count + EPSILON)
    image_norm = jnp.sqrt(image_sq_total / cell_count + EPSILON)
    velocity = STEP_LENGTH * mean_velocity / velocity_norm
    slope_z = (padded_mean[2:] - padded_mean[:-2]) * 0.5
    padded_x = jnp.pad(mean_image, ((0, 0), (1, 1), (0, 0)))
    slope_x = (padded_x[:, 2:] - padded_x[:, :-2]) * 0.5
    padded_y = jnp.pad(mean_image, ((0, 0), (0, 0), (1, 1)))
    slope_y = (padded_y[:, :, 2:] - padded_y[:, :, :-2]) * 0.5
    advected = velocity[:, 0] * slope_z + velocity[:, 1] * slope_x + velocity[:, 2] * slope_y
    new_template = (mean_image - advected) / image_norm
    similarity = cc_total / (subject_count * cell_count)
    return (velocity, new_template, similarity)


def solution(mesh):
    placed = (P("sub", None, None), P(("grp", "sub"), None, None, None))
    return jax.shard_map(
        on_device,
        mesh=mesh,
        in_specs=placed,
        out_specs=(P("sub", None, None, None), P("sub", None, None), P()),
        check_vma=False,
    )
```

profile of v0, /device:TPU:0, one launch (start us, length us, event | category | flops | bytes accessed | tf_op | source)
XLA Modules:
  0.0 629.7 jit_solution(13296579872331120941)
XLA Ops:
  7.9 5.9 fusion.30
  13.9 6.3 copy.25
  20.1 9.0 %convolution_bitcast_fusion.1 = f32[96,96,128]{1,0,2:T(8,128)} fusion(f32[96,96,128]{1,0,2:T(8,128)} %copy.25), kind=kOutput, calls=%fused_computation.46 | convolution fusion | flops 1358991360 | bytes 9437184 | tf_op jit(solution)/shard_map/ab,zby->zay/dot_general | solution.py:47
  29.1 6.4 %copy.26 = f32[96,96,128]{2,0,1:T(8,128)} copy(f32[96,96,128]{1,0,2:T(8,128)} %convolution_bitcast_fusion.1) | data formatting | bytes 9437184 | tf_op jit(solution)/shard_map/ab,zby->zay/transpose | solution.py:47
  39.5 6.0 fusion.81
  45.4 19.6 %all-gather.3.cloned.1.call-done = bf16[96,96,128]{2,1,0:T(8,128)(2,1)} async-done(((bf16[12,96,128]{2,1,0:T(8,128)(2,1)}), bf16[96,96,128]{2,1,0:T(8,128)(2,1)}) %all-gather.3.cloned.1.call-update) | async-done | bytes 2359312 | tf_op jit(solution)/shard_map/all_gather | solution.py:64
  68.8 7.6 %fusion.17 = f32[96,96,128]{2,1,0:T(8,128)S(1)} fusion(f32[96,96,128]{2,0,1:T(8,128)S(1)} %get-tuple-element.21), kind=kOutput, calls=%fused_computation.30 | convolution fusion | flops 1812004864 | bytes 9437184 | tf_op jit(solution)/shard_map/dot_general | solution.py:46
  76.4 17.3 %convolution_bitcast_fusion.3 = f32[96,96,128]{2,1,0:T(8,128)S(1)} fusion(f32[96,96,128]{2,1,0:T(8,128)S(1)} %fusion.17), kind=kOutput, calls=%fused_computation.52 | convolution fusion | flops 1358991360 | bytes 9437184 | tf_op jit(solution)/shard_map/ab,zby->zay/dot_general | solution.py:47
  93.7 9.9 %fusion.15 = f32[96,96,128]{2,0,1:T(8,128)} fusion(f32[96,96,128]{2,1,0:T(8,128)S(1)} %convolution_bitcast_fusion.3), kind=kOutput, calls=%fused_computation.28 | convolution fusion | flops 1358991360 | bytes 9437184 | tf_op jit(solution)/shard_map/ab,bxy->axy/dot_general | solution.py:50
  103.6 7.6 %fusion.21 = f32[96,96,128]{2,1,0:T(8,128)S(1)} fusion(f32[96,96,128]{2,0,1:T(8,128)S(1)} %get-tuple-element.23), kind=kOutput, calls=%fused_computation.34 | convolution fusion | flops 1812004864 | bytes 9437184 | tf_op jit(solution)/shard_map/dot_general | solution.py:46
  111.2 5.1 convolution_bitcast_fusion.4
  116.3 9.9 %fusion.19 = f32[96,96,128]{2,0,1:T(8,128)} fusion(f32[96,96,128]{2,1,0:T(8,128)S(1)} %convolution_bitcast_fusion.4), kind=kOutput, calls=%fused_computation.32 | convolution fusion | flops 1358991360 | bytes 9437184 | tf_op jit(solution)/shard_map/ab,bxy->axy/dot_general | solution.py:50
  126.2 7.6 %fusion.25 = f32[96,96,128]{2,1,0:T(8,128)S(1)} fusion(f32[96,96,128]{2,0,1:T(8,128)S(1)} %get-tuple-element.22), kind=kOutput, calls=%fused_computation.38 | convolution fusion | flops 1812004864 | bytes 9437184 | tf_op jit(solution)/shard_map/dot_general | solution.py:46
  133.8 6.1 convolution_bitcast_fusion.6
  143.6 6.3 copy.22
  149.9 8.9 %convolution_bitcast_fusion.2 = f32[96,96,128]{1,0,2:T(8,128)} fusion(f32[96,96,128]{1,0,2:T(8,128)} %copy.22), kind=kOutput, calls=%fused_computation.47 | convolution fusion | flops 1358991360 | bytes 9437184 | tf_op jit(solution)/shard_map/ab,zby->zay/dot_general | solution.py:47
  158.8 6.2 copy.23
  165.1 8.8 %fusion.84 = f32[96,96,128]{2,0,1:T(8,128)} fusion(f32[96,96,128]{2,0,1:T(8,128)} %copy.23), kind=kOutput, calls=%fused_computation.119 | convolution fusion | flops 1358991360 | bytes 9437184 | tf_op jit(solution)/shard_map/ab,bxy->axy/dot_general | solution.py:50
  174.7 7.3 %fusion.8 = (f32[96,1,96,128]{3,0,2,1:T(8,128)}, f32[96,1,96,128]{3,0,2,1:T(8,128)}, f32[96,1,96,128]{3,0,2,1:T(8,128)}) fusion(f32[96,96,128]{2,0,1:T(8,128)S(1)} %copy_convert_fusion), kind=kLoop, calls=%fused_computation.21 | loop fusion | flops 7077888 | bytes 18874368 | tf_op jit(solution)/shard_map/stack | solution.py:60
  182.0 21.9 %fusion.27 = (f32[]{:T(128)}, f32[96,96,128]{2,0,1:T(8,128)}) fusion(f32[96,96,128]{2,0,1:T(8,128)} %fusion.84, f32[96,96,128]{2,0,1:T(8,128)} %fusion.81, f32[96,96,128]{2,0,1:T(8,128)} %fusion.15, f32[96,96,128]{2,0,1:T(8,128)} %fusion.19, bf16[96,96,128]{2,1,0:T(8,128)(2,1)S(1)} %copy-done.2, bf16[1,96,96,128]{3,2,1,0:T(8,128)(2,1)S(1)} %copy-done, ...), kind=kOutput, calls=%fused_computation.44 | convolution fusion | flops 1384943616 | bytes 33030148 | tf_op jit(solution)/shard_map/ab,bxy->axy/dot_general | solution.py:50
  203.9 5.2 maximum_multiply_fusion
  209.1 22.3 %fusion.2 = f32[96,3,96,128]{3,2,1,0:T(8,128)S(1)} fusion(f32[96,3,96,128]{3,0,2,1:T(8,128)S(1)} %maximum_multiply_fusion), kind=kOutput, calls=%fused_computation.11 | convolution fusion | flops 5435965440 | bytes 28311552 | tf_op jit(solution)/shard_map/zcxb,ba->zcxa/dot_general | solution.py:92
  231.4 15.8 %convolution_bitcast_fusion = f32[96,3,96,128]{3,2,1,0:T(8,128)} fusion(f32[96,3,96,128]{3,2,1,0:T(8,128)S(1)} %fusion.2), kind=kOutput, calls=%fused_computation.13 | convolution fusion | flops 4076946432 | bytes 28311552 | tf_op jit(solution)/shard_map/ab,zcby->zcay/dot_general | solution.py:95
  247.2 25.3 %fusion = f32[96,3,96,128]{3,0,2,1:T(8,128)S(1)} fusion(f32[96,3,96,128]{3,2,1,0:T(8,128)} %convolution_bitcast_fusion), kind=kOutput, calls=%fused_computation.9 | convolution fusion | flops 4076946432 | bytes 28311552 | tf_op jit(solution)/shard_map/ab,bcxy->acxy/dot_general | solution.py:100
  272.6 7.0 %pad_maximum_fusion = f32[96,4,96,128]{3,0,2,1:T(8,128)} fusion(f32[96,1,96,128]{3,0,2,1:T(8,128)S(1)} %bitcast.124, f32[96,3,96,128]{3,0,2,1:T(8,128)S(1)} %fusion), kind=kLoop, calls=%fused_computation.7 | loop fusion | flops 4718592 | bytes 37748736 | tf_op jit(solution)/shard_map/concatenate | solution.py:103
  279.6 7.3 %copy.40 = f32[96,4,96,128]{3,0,1,2:T(8,128)S(1)} copy(f32[96,4,96,128]{3,0,2,1:T(8,128)} %pad_maximum_fusion) | data formatting | bytes 37748736
  286.9 13.1 %copy.75 = f32[12,8,384,128]{3,1,2,0:T(8,128)} copy(f32[12,8,384,128]{3,2,1,0:T(8,128)S(1)} %bitcast.122) | data formatting | bytes 37748736
  300.1 138.1 %reduce-scatter.8.cloned.1.call-done = f32[24,49152]{1,0:T(8,128)} async-done(((f32[96,49152]{1,0:T(8,128)}), f32[24,49152]{1,0:T(8,128)}) %reduce-scatter.8.cloned.1.call-update) | async-done | bytes 4718608
  441.3 4.9 copy.34
  446.3 95.4 %reduce-scatter.6.cloned.1.call-done = f32[12,4,24,128]{3,2,1,0:T(8,128)} async-done(((f32[96,4,24,128]{3,2,1,0:T(8,128)}), f32[12,4,24,128]{3,2,1,0:T(8,128)}) %reduce-scatter.6.cloned.1.call-update) | async-done | bytes 589840 | tf_op jit(solution)/shard_map/reduce_scatter | solution.py:105
  541.7 40.6 %psum.23 = f32[]{:T(128)} all-reduce(f32[]{:T(128)} %get-tuple-element.14), channel_id=1, replica_groups=mesh['grp'=4,'sub'=8] {'grp','sub'}, use_global_device_ids=true, to_apply=%region_7.8 | all-reduce | flops 1 | bytes 8 | tf_op jit(solution)/shard_map/psum | solution.py:112
  587.3 21.7 %all-reduce.3 = (f32[]{:T(128)}, f32[]{:T(128)}) all-reduce(f32[]{:T(128)} %multiply_reduce_fusion, f32[]{:T(128)} %multiply_reduce_fusion.1), channel_id=1, replica_groups=mesh['grp'=4,'sub'=8] {'sub'}, use_global_device_ids=true, to_apply=%region_3.4 | all-reduce | flops 2 | bytes 16 | tf_op jit(solution)/shard_map/psum | solution.py:113
  (42 shorter events, 31.9 us)
Async XLA Ops:
  7.2 57.8 %all-gather.3.cloned.1.call-start = ((), (), s32[]{:S(2)}) async-start(), calls=%async_computation.2 | async-start | bytes 2654208 | tf_op jit(solution)/shard_map/all_gather | solution.py:64
  7.9 430.3 %reduce-scatter.8.cloned.1.call-start = ((), (), s32[]{:S(2)}) async-start(), calls=%async_computation.5 | async-start | bytes 23592960
  29.1 6.4 %copy-start = (bf16[1,96,96,128]{3,2,1,0:T(8,128)(2,1)S(1)}, bf16[1,96,96,128]{3,2,1,0:T(8,128)(2,1)}, u32[]{:S(2)}) copy-start(bf16[1,96,96,128]{3,2,1,0:T(8,128)(2,1)} %param.3) | copy-start | bytes 7077892
  35.5 3.9 copy-start.3
  133.8 6.1 copy-start.1
  165.1 8.8 %copy-start.2 = (bf16[96,96,128]{2,1,0:T(8,128)(2,1)S(1)}, bf16[96,96,128]{2,1,0:T(8,128)(2,1)}, u32[]{:S(2)}) copy-start(bf16[96,96,128]{2,1,0:T(8,128)(2,1)} %all-gather.3.cloned.1.call-done) | copy-start | bytes 7077892
  182.0 21.9 %copy-start.4 = (f32[96,1,96,128]{3,0,2,1:T(8,128)S(1)}, f32[96,1,96,128]{3,0,2,1:T(8,128)}, u32[]{:S(2)}) copy-start(f32[96,1,96,128]{3,0,2,1:T(8,128)} %get-tuple-element.16) | copy-start | bytes 14155780
  182.0 21.9 %copy-start.5 = (f32[96,1,96,128]{3,0,2,1:T(8,128)S(1)}, f32[96,1,96,128]{3,0,2,1:T(8,128)}, u32[]{:S(2)}) copy-start(f32[96,1,96,128]{3,0,2,1:T(8,128)} %get-tuple-element.17) | copy-start | bytes 14155780
  231.4 41.2 %slice-start = ((s8[4718592]{0:T(1024)(128)(4,1)}), s8[4194304]{0:T(1024)(128)(4,1)S(1)}, s32[]{:S(2)}) async-start(s8[4718592]{0:T(1024)(128)(4,1)} %bitcast.123), calls=%async_computation.6 | async-start | bytes 8388608
  247.2 25.3 %slice-start.1 = ((s8[4718592]{0:T(1024)(128)(4,1)}), s8[524288]{0:T(1024)(128)(4,1)S(1)}, s32[]{:S(2)}) async-start(s8[4718592]{0:T(1024)(128)(4,1)} %bitcast.123), calls=%async_computation.7 | async-start | bytes 1048576
  300.0 241.6 %reduce-scatter.6.cloned.1.call-start = ((), (), s32[]{:S(2)}) async-start(), calls=%async_computation.3 | async-start | bytes 5308416 | tf_op jit(solution)/shard_map/reduce_scatter | solution.py:105
  446.2 136.1 %all-gather.5.cloned.1.call-start = ((), (), s32[]{:S(2)}) async-start(), calls=%async_computation.4 | async-start | bytes 2949120 | tf_op jit(solution)/shard_map/all_gather | solution.py:106
  610.9 9.6 %collective-permute-start = (f32[1,96,128]{2,1,0:T(8,128)S(1)}, f32[1,96,128]{2,1,0:T(8,128)S(1)}, u32[]{:S(2)}, u32[]{:S(2)}) collective-permute-start(f32[1,96,128]{2,1,0:T(8,128)S(1)} %get-tuple-element.24), channel_id=1, source_target_pairs={{1,0},{2,1},{3,2},{4,3},{5,4},{6,5},{7,6},{9,8},{10,9},{11,10},{12... | collective-permute-start | bytes 147464 | tf_op jit(solution)/shard_map/ppermute | solution.py:26
  612.2 8.3 %collective-permute-start.1 = (f32[1,96,128]{2,1,0:T(8,128)S(1)}, f32[1,96,128]{2,1,0:T(8,128)S(1)}, u32[]{:S(2)}, u32[]{:S(2)}) collective-permute-start(f32[1,96,128]{2,1,0:T(8,128)S(1)} %get-tuple-element.25), channel_id=1, source_target_pairs={{0,1},{1,2},{2,3},{3,4},{4,5},{5,6},{6,7},{8,9},{9,10},{10,11},{11... | collective-permute-start | bytes 147464 | tf_op jit(solution)/shard_map/ppermute | solution.py:25
Sparse Core Ops, SparseCore 0:
  10.2 54.7 all-gather.2
  300.1 137.9 reduce-scatter.7
  446.3 95.2 reduce-scatter.5
  543.1 23.9 all-gather.4
where the time goes:
time: 631 us; the launch traced here: 630 us
  waiting for transfers between devices  254 us (40%)
  matrix products  199 us (32%)
  blocking collectives  62.4 us (10%)
  local copies, waits for them, and re-layouts  55.8 us (9%)
  other arithmetic  35.7 us (6%)
  between operations  17.4 us (3%)
    unnamed x5, waiting for transfers between devices  139 us
    reduce_scatter x1, waiting for transfers between devices, on_device(): lax.psum_scatter(group_part, 'sub', scatter_dimension=0, tiled=True)  95.4 us
    dot_general x5, matrix products, filter_volume(): jnp.einsum('ab,bxy->axy', along_z, result, precision=HIGH, preferred_elem...  56.5 us
    dot_general x5, matrix products, filter_volume(): jnp.einsum('ab,zby->zay', along_x, result, precision=HIGH, preferred_elem...  46.5 us
    psum x1, blocking collectives, on_device(): cc_total = lax.psum(cc_local, ('grp', 'sub'))  40.6 us
    dot_general x5, matrix products, filter_volume(): jnp.dot(volume, along_y, precision=HIGH, preferred_element_type=jnp.float32)  32.2 us
    unnamed x20, local copies, waits for them, and re-layouts  25.7 us
    dot_general x1, matrix products, on_device(): jnp.einsum('ab,bcxy->acxy', gauss_z, planar, precision=HIGH, preferred_el...  25.3 us
  transfers between devices with their start and end apart: 6, of which 3 were waited for; matrix products, arithmetic and copies ran while one was open for 6% of the time, Pallas kernels for 0%

commit v1 on v0

v1 whole, which is shorter than its diff:
```python
import math

import jax
import jax.numpy as jnp
from jax import lax
from jax.experimental import pallas as pl
from jax.experimental.pallas import tpu as pltpu
from jax.sharding import PartitionSpec as P

RADIUS = 4
REACH = 5


EPSILON = 1e-05
STEP_LENGTH = 0.5
VARIANCE = 3.0
HIGH = lax.Precision.HIGHEST


def band_matrix(length, extent, weighted):
    row_ids = lax.broadcasted_iota(jnp.int32, (length, length), 0)
    col_ids = lax.broadcasted_iota(jnp.int32, (length, length), 1)
    inside = jnp.abs(row_ids - col_ids) <= extent
    if weighted:
        offset_f = (row_ids - col_ids).astype(jnp.float32)
        total = sum(math.exp(-o * o / (2.0 * VARIANCE)) for o in range(-extent, extent + 1))
        values = jnp.exp(-offset_f * offset_f / (2.0 * VARIANCE)) / total
        return jnp.where(inside, values, 0.0)
    return jnp.where(inside, 1.0, 0.0).astype(jnp.bfloat16)


def gauss_weights(extent):
    raw = [math.exp(-o * o / (2.0 * VARIANCE)) for o in range(-extent, extent + 1)]
    return [w / sum(raw) for w in raw]


def split_dot(field, band):
    high = field.astype(jnp.bfloat16)
    low = (field - high.astype(jnp.float32)).astype(jnp.bfloat16)
    return jnp.dot(high, band, preferred_element_type=jnp.float32) + jnp.dot(
        low, band, preferred_element_type=jnp.float32
    )


def window_x(plane):
    rows, lanes = plane.shape
    zeros = jnp.zeros((8, lanes), jnp.float32)
    padded = jnp.concatenate([zeros, plane, zeros], axis=0)
    two = padded + pltpu.roll(padded, 1, 0)
    four = two + pltpu.roll(two, 2, 0)
    nine = four + pltpu.roll(four, 4, 0) + pltpu.roll(padded, 8, 0)
    return pltpu.roll(nine, rows + 16 - RADIUS, 0)[8 : 8 + rows]


def factor_kernel(i_ref, j_ref, band_ref, f_ref, cc_ref, sums):
    depth, rows, lanes = i_ref.shape
    chunk = 4
    band = band_ref[...]
    edge = jnp.zeros((RADIUS, rows, lanes), jnp.float32)
    for k in range(5):
        sums[k, :RADIUS] = edge
        sums[k, depth + RADIUS :] = edge
    cc_ref[...] = jnp.zeros_like(cc_ref)

    @pl.loop(0, depth // chunk)
    def _(step):
        z = step * chunk
        i16 = i_ref[pl.ds(z, chunk)].reshape(chunk * rows, lanes)
        j16 = j_ref[pl.ds(z, chunk)].reshape(chunk * rows, lanes)
        i32, j32 = i16.astype(jnp.float32), j16.astype(jnp.float32)
        fields = (
            jnp.dot(i16, band, preferred_element_type=jnp.float32),
            split_dot(i32 * i32, band),
            jnp.dot(j16, band, preferred_element_type=jnp.float32),
            split_dot(j32 * j32, band),
            split_dot(i32 * j32, band),
        )
        for k, field in enumerate(fields):
            sums[k, pl.ds(z + RADIUS, chunk)] = field.reshape(chunk, rows, lanes)

    scale = 1.0 / (2 * RADIUS + 1) ** 3

    @pl.loop(0, depth // chunk)
    def _(step):
        z = step * chunk
        planes = []
        for k in range(5):
            a = [sums[k, z + o] for o in range(chunk + 2 * RADIUS)]
            mid = ((a[3] + a[4]) + (a[5] + a[6])) + (a[7] + a[8])
            p, q = a[1] + a[2], a[9] + a[10]
            outs = (mid + (a[0] + p), mid + (p + a[9]), mid + (a[2] + q), mid + (q + a[11]))
            planes.append([window_x(o) * scale for o in outs])
        for c in range(chunk):
            mean_i, mean_ii, mean_j, mean_jj, mean_ij = (planes[k][c] for k in range(5))
            i32 = i_ref[z + c].astype(jnp.float32)
            j32 = j_ref[z + c].astype(jnp.float32)
            cross = mean_ij - mean_i * mean_j
            var_i = mean_ii - mean_i * mean_i
            var_j = mean_jj - mean_j * mean_j
            ratio = cross / (var_i * var_j + EPSILON)
            slope = cross / (var_i + EPSILON)
            f_ref[z + c] = 2.0 * ratio * (j32 - mean_j - slope * (i32 - mean_i))
            cc_ref[...] += cross * ratio


def factors(image, moving):
    depth, rows, lanes = image.shape
    cells = depth * rows * lanes
    vmem = pl.BlockSpec(memory_space=pltpu.VMEM)
    return pl.pallas_call(
        factor_kernel,
        out_shape=(
            jax.ShapeDtypeStruct((depth, rows, lanes), jnp.float32),
            jax.ShapeDtypeStruct((rows, lanes), jnp.float32),
        ),
        in_specs=[vmem] * 3,
        out_specs=(vmem, vmem),
        scratch_shapes=[pltpu.VMEM((5, depth + 2 * RADIUS, rows, lanes), jnp.float32)],
        compiler_params=pltpu.CompilerParams(vmem_limit_bytes=56 * 2**20),
        cost_estimate=pl.CostEstimate(
            flops=cells * lanes * 16, bytes_accessed=cells * 60, transcendentals=2 * cells
        ),
    )(image, moving, band_matrix(lanes, RADIUS, False))


def with_halo(slab, width):
    devices, length = lax.axis_size("sub"), slab.shape[0]
    before, after = [], []
    hop, left = 1, width
    while left > 0:
        take = min(left, length)
        up = [(i, i + hop) for i in range(devices - hop)]
        down = [(j, i) for i, j in up]
        before.insert(0, lax.ppermute(slab[length - take :], "sub", up))
        after.append(lax.ppermute(slab[:take], "sub", down))
        hop, left = hop + 1, left - take
    return jnp.concatenate(before + [slab] + after, axis=0)


def reduced(volume):
    part = lax.psum_scatter(volume, "grp", scatter_dimension=1, tiled=True)
    part = lax.psum_scatter(part, "sub", scatter_dimension=0, tiled=True)
    return lax.all_gather(part, "grp", axis=1, tiled=True)


def on_device(template, subjects):
    image = lax.all_gather(template, "sub", axis=0, tiled=True)
    depth, height, width = image.shape
    slab = template.shape[0]
    subject_count = subjects.shape[0] * lax.axis_size("grp") * lax.axis_size("sub")
    cell_count = depth * height * width
    mean_image = reduced(subjects[0].astype(jnp.float32)) / subject_count
    padded_mean = with_halo(mean_image, 1)
    factor, cc = factors(image, subjects[0])
    cc_local = jnp.sum(cc)
    total = with_halo(reduced(factor), REACH)

    reach = REACH + 1
    padded = jnp.pad(image, ((reach, reach), (0, 0), (0, 0)))
    near = lax.dynamic_slice_in_dim(padded, lax.axis_index("sub") * slab, slab + 2 * reach, axis=0)
    near = jnp.pad(near.astype(jnp.float32), ((0, 0), (1, 1), (1, 1)))
    slopes = (
        (near[2:, 1:-1, 1:-1] - near[:-2, 1:-1, 1:-1]) * 0.5,
        (near[1:-1, 2:, 1:-1] - near[1:-1, :-2, 1:-1]) * 0.5,
        (near[1:-1, 1:-1, 2:] - near[1:-1, 1:-1, :-2]) * 0.5,
    )
    weights = gauss_weights(REACH)
    along_z = []
    for slope in slopes:
        force = total * slope
        along_z.append(sum(w * force[o : o + slab] for o, w in enumerate(weights)))
    smooth = jnp.stack(along_z, axis=1)
    gauss_x = band_matrix(height, REACH, True)
    gauss_y = band_matrix(width, REACH, True)
    smooth = jnp.einsum(
        "zcxb,ba->zcxa", smooth, gauss_y, precision=HIGH, preferred_element_type=jnp.float32
    )
    smooth = jnp.einsum(
        "ab,zcby->zcay", gauss_x, smooth, precision=HIGH, preferred_element_type=jnp.float32
    )
    mean_velocity = smooth / subject_count
    velocity_square = jnp.sum(mean_velocity * mean_velocity)
    image_square = jnp.sum(mean_image * mean_image)
    groups = lax.axis_size("grp")
    sums = lax.psum(
        jnp.stack([cc_local, velocity_square / groups, image_square / groups]), ("grp", "sub")
    )
    velocity_norm = jnp.sqrt(sums[1] / cell_count + EPSILON)
    image_norm = jnp.sqrt(sums[2] / cell_count + EPSILON)
    velocity = STEP_LENGTH * mean_velocity / velocity_norm
    slope_z = (padded_mean[2:] - padded_mean[:-2]) * 0.5
    padded_x = jnp.pad(mean_image, ((0, 0), (1, 1), (0, 0)))
    slope_x = (padded_x[:, 2:] - padded_x[:, :-2]) * 0.5
    padded_y = jnp.pad(mean_image, ((0, 0), (0, 0), (1, 1)))
    slope_y = (padded_y[:, :, 2:] - padded_y[:, :, :-2]) * 0.5
    advected = velocity[:, 0] * slope_z + velocity[:, 1] * slope_x + velocity[:, 2] * slope_y
    new_template = (mean_image - advected) / image_norm
    similarity = sums[0] / (subject_count * cell_count)
    return (velocity, new_template, similarity)


def solution(mesh):
    placed = (P("sub", None, None), P(("grp", "sub"), None, None, None))
    return jax.shard_map(
        on_device,
        mesh=mesh,
        in_specs=placed,
        out_specs=(P("sub", None, None, None), P("sub", None, None), P()),
        check_vma=False,
    )
```

time: 631 us -> 369 us (0.58)
  matrix products: 199 us -> 4.12 us
  local copies, waits for them, and re-layouts: 55.8 us -> 3.37 us
  Pallas kernels: 0 us -> 32.6 us
  other arithmetic: 35.7 us -> 11.4 us
  waiting for transfers between devices: 254 us -> 232 us
  blocking collectives: 62.4 us -> 54.9 us
    dot_general x18 -> x2, matrix products: 199 us -> 4.12 us  [the longest x1 2.56 us: on_device(): jnp.einsum('ab,zcby->zcay', gauss_x, smooth, precision=HIGH, preferred_el...]
    unnamed x5, waiting for transfers between devices: 139 us -> 1.2 us
    reduce_scatter x1 -> x4, waiting for transfers between devices: 95.4 us -> 171 us  [the longest x2 126 us: reduced(): part = lax.psum_scatter(part, 'sub', scatter_dimension=0, tiled=True)]
    pallas_call x0 -> x1, Pallas kernels: none -> 32.6 us  [factors(): pl.pallas_call(factor_kernel, out_shape=(jax.ShapeDtypeStruct((depth, row...]
    all_gather x2 -> x1, waiting for transfers between devices: 19.6 us -> 52.1 us  [on_device(): image = lax.all_gather(template, 'sub', axis=0, tiled=True)]
    unnamed x20 -> x9, local copies, waits for them, and re-layouts: 25.7 us -> 1.4 us
    psum x2 -> x1, blocking collectives: 62.4 us -> 39.5 us  [on_device(): lax.psum(jnp.stack([cc_local, velocity_square / groups, image_square / gr...]
    all_gather x0 -> x2, blocking collectives: none -> 15.4 us  [reduced(): return lax.all_gather(part, 'grp', axis=1, tiled=True)]
  transfers between devices with their start and end apart: 6 -> 9, of which waited for: 3 -> 5; matrix products, arithmetic and copies ran while one was open for 6% -> 4% of each run, Pallas kernels for 0% -> 9%
where the time goes in v1:
time: 369 us
  waiting for transfers between devices  232 us (63%)
  blocking collectives  54.9 us (15%)
  Pallas kernels  32.6 us (9%)
  between operations  20.3 us (6%)
  other arithmetic  11.4 us (3%)
  starting transfers between devices  9.94 us (3%)
  matrix products  4.12 us (1%)
    reduce_scatter x2, waiting for transfers between devices, reduced(): part = lax.psum_scatter(part, 'sub', scatter_dimension=0, tiled=True)  126 us
    all_gather x1, waiting for transfers between devices, on_device(): image = lax.all_gather(template, 'sub', axis=0, tiled=True)  52.1 us
    reduce_scatter x2, waiting for transfers between devices, reduced(): part = lax.psum_scatter(volume, 'grp', scatter_dimension=1, tiled=True)  45.8 us
    psum x1, blocking collectives, on_device(): lax.psum(jnp.stack([cc_local, velocity_square / groups, image_square / gr...  39.5 us
    pallas_call x1, Pallas kernels, factors(): pl.pallas_call(factor_kernel, out_shape=(jax.ShapeDtypeStruct((depth, row...  32.6 us
    all_gather x2, blocking collectives, reduced(): return lax.all_gather(part, 'grp', axis=1, tiled=True)  15.4 us
    ppermute x2, waiting for transfers between devices, with_halo(): before.insert(0, lax.ppermute(slab[length - take:], 'sub', up))  7.74 us
  transfers between devices with their start and end apart: 9, of which 5 were waited for; matrix products, arithmetic and copies ran while one was open for 4% of the time, Pallas kernels for 9%

profile of v1, /device:TPU:0, one launch (start us, length us, event | category | flops | bytes accessed | tf_op | source)
XLA Modules:
  0.0 369.0 jit_solution(14819082039107364865)
XLA Ops:
  8.0 0.7 all-gather.2.cloned.1.call-update
  8.8 4.5 %bitcast_convert_fusion = f32[96,96,128]{2,1,0:T(8,128)} fusion(bf16[1,96,96,128]{3,2,1,0:T(8,128)(2,1)} %param.3), kind=kLoop, calls=%fused_computation.148 | loop fusion | flops 1179648 | bytes 7077888 | tf_op jit(solution)/shard_map/convert_element_type | solution.py:152
  13.3 0.6 select_convert_fusion.band_ref
  14.0 52.1 %all-gather.2.cloned.1.call-done.i_ref = bf16[96,96,128]{2,1,0:T(8,128)(2,1)} async-done(((bf16[12,96,128]{2,1,0:T(8,128)(2,1)}), bf16[96,96,128]{2,1,0:T(8,128)(2,1)}) %all-gather.2.cloned.1.call-update) | async-done | bytes 2359312 | tf_op jit(solution)/shard_map/all_gather | solution.py:147
  66.1 32.6 %shard_map.49 = (f32[96,96,128]{2,1,0:T(8,128)}, f32[96,128]{1,0:T(8,128)}) custom-call(bf16[96,96,128]{2,1,0:T(8,128)(2,1)} %all-gather.2.cloned.1.call-done.i_ref, bf16[96,96,128]{2,1,0:T(8,128)(2,1)} %bitcast.41, bf16[128,128]{1,0:T(8,128)(2,1)} %select_convert_fusion.band_ref), custom_call_target="tpu_custom_call" | custom-call | flops 2415919104 | bytes 70778880 | tf_op jit(solution)/shard_map/pallas_call | solution.py:110
  98.7 0.5 reduce-scatter.11.cloned.1.call-update
  99.3 45.8 %reduce-scatter.5.cloned.1.call-done = f32[96,24,128]{2,1,0:T(8,128)} async-done(((f32[96,96,128]{2,1,0:T(8,128)}), f32[96,24,128]{2,1,0:T(8,128)}) %reduce-scatter.5.cloned.1.call-update) | async-done | bytes 1179664 | tf_op jit(solution)/shard_map/reduce_scatter | solution.py:141
  145.1 0.6 reduce_sum.27
  145.8 66.7 %reduce-scatter.11.cloned.1.call-done = f32[12,24,128]{2,1,0:T(8,128)} async-done(((f32[96,24,128]{2,1,0:T(8,128)}), f32[12,24,128]{2,1,0:T(8,128)}) %reduce-scatter.11.cloned.1.call-update) | async-done | bytes 147472 | tf_op jit(solution)/shard_map/reduce_scatter | solution.py:142
  212.5 7.7 %all_gather.11 = f32[12,96,128]{2,1,0:T(8,128)S(1)} all-gather(f32[12,24,128]{2,1,0:T(8,128)} %reduce-scatter.11.cloned.1.call-done), channel_id=1, replica_groups=mesh['grp'=4,'sub'=8] {'grp'}, dimensions={1}, use_global_device_ids=true | all-gather | bytes 737280 | tf_op jit(solution)/shard_map/all_gather | solution.py:143
  220.2 58.9 %reduce-scatter.7.cloned.1.call-done = f32[12,24,128]{2,1,0:T(8,128)} async-done(((f32[96,24,128]{2,1,0:T(8,128)}), f32[12,24,128]{2,1,0:T(8,128)}) %reduce-scatter.7.cloned.1.call-update) | async-done | bytes 147472 | tf_op jit(solution)/shard_map/reduce_scatter | solution.py:142
  279.1 7.7 %all_gather.10 = f32[12,96,128]{2,1,0:T(8,128)S(1)} all-gather(f32[12,24,128]{2,1,0:T(8,128)} %reduce-scatter.7.cloned.1.call-done), channel_id=1, replica_groups=mesh['grp'=4,'sub'=8] {'grp'}, dimensions={1}, use_global_device_ids=true | all-gather | bytes 737280 | tf_op jit(solution)/shard_map/all_gather | solution.py:143
  286.9 0.7 fusion.98
  287.6 2.9 collective-permute-start
  290.5 0.8 broadcast_multiply_fusion
  291.3 1.3 collective-permute-start.1
  292.6 0.6 fusion.97
  293.2 1.3 collective-permute-start.2
  295.1 7.7 %collective-permute-done = f32[5,96,128]{2,1,0:T(8,128)S(1)} collective-permute-done((f32[5,96,128]{2,1,0:T(8,128)}, f32[5,96,128]{2,1,0:T(8,128)S(1)}, u32[]{:S(2)}, u32[]{:S(2)}) %collective-permute-start) | collective-permute-done | bytes 245792 | tf_op jit(solution)/shard_map/ppermute | solution.py:134
  303.0 0.7 fusion.11
  303.7 0.4 fusion.27
  304.1 0.4 fusion.38
  304.4 0.4 fusion.49
  304.8 1.6 fusion
  306.4 2.6 multiply_reduce_fusion
  309.6 0.7 pad_maximum_fusion.3
  310.3 4.2 %collective-permute-start.3 = (f32[1,96,128]{2,1,0:T(8,128)S(1)}, f32[1,96,128]{2,1,0:T(8,128)S(1)}, u32[]{:S(2)}, u32[]{:S(2)}) collective-permute-start(f32[1,96,128]{2,1,0:T(8,128)S(1)} %copy-done.2), channel_id=1, source_target_pairs={{0,1},{1,2},{2,3},{3,4},{4,5},{5,6},{6,7},{8,9},{9,10},{10,11},{11... | collective-permute-start | bytes 147464 | tf_op jit(solution)/shard_map/ppermute | solution.py:134
  314.6 39.5 %psum.7 = f32[3]{0:T(128)S(1)} all-reduce(f32[3]{0:T(128)S(1)} %pad_maximum_fusion.3), channel_id=1, replica_groups=mesh['grp'=4,'sub'=8] {'grp','sub'}, use_global_device_ids=true, to_apply=%region_7.8 | all-reduce | flops 3 | bytes 24 | tf_op jit(solution)/shard_map/psum | solution.py:185
  354.0 0.6 fusion.99
  355.3 0.2 fusion.3
  356.2 1.3 copy.8
  358.2 2.1 fusion.18
  (22 shorter events, 0.5 us)
Async XLA Ops:
  8.0 58.1 %all-gather.2.cloned.1.call-start = ((), (), s32[]{:S(2)}) async-start(), calls=%async_computation.4 | async-start | bytes 2654208 | tf_op jit(solution)/shard_map/all_gather | solution.py:147
  8.7 90.0 %reduce-scatter.9.cloned.1.call-start = ((), (), s32[]{:S(2)}) async-start(), calls=%async_computation.7 | async-start | bytes 5898240 | tf_op jit(solution)/shard_map/reduce_scatter | solution.py:141
  13.3 131.8 %reduce-scatter.5.cloned.1.call-start = ((), (), s32[]{:S(2)}) async-start(), calls=%async_computation.5 | async-start | bytes 5898240 | tf_op jit(solution)/shard_map/reduce_scatter | solution.py:141
  98.6 113.9 %reduce-scatter.11.cloned.1.call-start = ((), (), s32[]{:S(2)}) async-start(), calls=%async_computation.8 | async-start | bytes 1327104 | tf_op jit(solution)/shard_map/reduce_scatter | solution.py:142
  98.7 46.4 %copy-start.1 = (f32[96,128]{1,0:T(8,128)S(1)}, f32[96,128]{1,0:T(8,128)}, u32[]{:S(2)}) copy-start(f32[96,128]{1,0:T(8,128)} %get-tuple-element.6) | copy-start | bytes 147460
  98.7 47.0 %copy-start = (bf16[96,96,128]{2,1,0:T(8,128)(2,1)S(1)}, bf16[96,96,128]{2,1,0:T(8,128)(2,1)}, u32[]{:S(2)}) copy-start(bf16[96,96,128]{2,1,0:T(8,128)(2,1)} %all-gather.2.cloned.1.call-done.i_ref) | copy-start | bytes 7077892
  99.2 179.9 %reduce-scatter.7.cloned.1.call-start = ((), (), s32[]{:S(2)}) async-start(), calls=%async_computation.6 | async-start | bytes 1327104 | tf_op jit(solution)/shard_map/reduce_scatter | solution.py:142
  287.6 15.3 %collective-permute-start = (f32[5,96,128]{2,1,0:T(8,128)}, f32[5,96,128]{2,1,0:T(8,128)S(1)}, u32[]{:S(2)}, u32[]{:S(2)}) collective-permute-start(f32[5,96,128]{2,1,0:T(8,128)} %get-tuple-element.21), channel_id=1, source_target_pairs={{0,1},{1,2},{2,3},{3,4},{4,5},{5,6},{6,7},{8,9},{9,10},{10,11},{11... | collective-permute-start | bytes 737288 | tf_op jit(solution)/shard_map/ppermute | solution.py:134
  291.3 11.7 %collective-permute-start.1 = (f32[5,96,128]{2,1,0:T(8,128)S(1)}, f32[5,96,128]{2,1,0:T(8,128)S(1)}, u32[]{:S(2)}, u32[]{:S(2)}) collective-permute-start(f32[5,96,128]{2,1,0:T(8,128)S(1)} %get-tuple-element.20), channel_id=1, source_target_pairs={{1,0},{2,1},{3,2},{4,3},{5,4},{6,5},{7,6},{9,8},{10,9},{11,10},{12... | collective-permute-start | bytes 737288 | tf_op jit(solution)/shard_map/ppermute | solution.py:135
  293.2 64.9 %collective-permute-start.2 = (f32[1,96,128]{2,1,0:T(8,128)}, f32[1,96,128]{2,1,0:T(8,128)}, u32[]{:S(2)}, u32[]{:S(2)}) collective-permute-start(f32[1,96,128]{2,1,0:T(8,128)} %get-tuple-element.16), channel_id=1, source_target_pairs={{1,0},{2,1},{3,2},{4,3},{5,4},{6,5},{7,6},{9,8},{10,9},{11,10},{12... | collective-permute-start | bytes 147464 | tf_op jit(solution)/shard_map/ppermute | solution.py:135
  306.4 3.9 %copy-start.2 = (f32[1,96,128]{2,1,0:T(8,128)S(1)}, f32[1,96,128]{2,1,0:T(8,128)}, u32[]{:S(2)}) copy-start(f32[1,96,128]{2,1,0:T(8,128)} %get-tuple-element.17) | copy-start | bytes 147460
  310.3 47.9 %collective-permute-start.3 = (f32[1,96,128]{2,1,0:T(8,128)S(1)}, f32[1,96,128]{2,1,0:T(8,128)S(1)}, u32[]{:S(2)}, u32[]{:S(2)}) collective-permute-start(f32[1,96,128]{2,1,0:T(8,128)S(1)} %copy-done.2), channel_id=1, source_target_pairs={{0,1},{1,2},{2,3},{3,4},{4,5},{5,6},{6,7},{8,9},{9,10},{10,11},{11... | collective-permute-start | bytes 147464 | tf_op jit(solution)/shard_map/ppermute | solution.py:134
Sparse Core Ops, SparseCore 0:
  11.2 54.7 all-gather.1
Sparse Core Ops, SparseCore 1:
  13.4 50.4 reduce-scatter.8
  98.7 46.3 reduce-scatter.4
  148.3 64.1 reduce-scatter.10
  215.9 63.2 reduce-scatter.6

commit v2 on v1

--- a/solution.py
+++ b/solution.py
@@ -1,3 +1,4 @@
+import functools
 import math
 
 import jax
@@ -15,6 +16,7 @@
 STEP_LENGTH = 0.5
 VARIANCE = 3.0
 HIGH = lax.Precision.HIGHEST
+MESH = pl.DeviceIdType.MESH
 
 
 def band_matrix(length, extent, weighted):
@@ -123,24 +125,274 @@
     )(image, moving, band_matrix(lanes, RADIUS, False))
 
 
-def with_halo(slab, width):
-    devices, length = lax.axis_size("sub"), slab.shape[0]
-    before, after = [], []
-    hop, left = 1, width
-    while left > 0:
-        take = min(left, length)
-        up = [(i, i + hop) for i in range(devices - hop)]
-        down = [(j, i) for i, j in up]
-        before.insert(0, lax.ppermute(slab[length - take :], "sub", up))
-        after.append(lax.ppermute(slab[:take], "sub", down))
-        hop, left = hop + 1, left - take
-    return jnp.concatenate(before + [slab] + after, axis=0)
-
-
-def reduced(volume):
-    part = lax.psum_scatter(volume, "grp", scatter_dimension=1, tiled=True)
-    part = lax.psum_scatter(part, "sub", scatter_dimension=0, tiled=True)
-    return lax.all_gather(part, "grp", axis=1, tiled=True)
+def bits(size):
+    return [1 << k for k in range(size.bit_length() - 1)]
+
+
+def plan(groups, owners, order):
+    offsets, steps = list(range(owners)), []
+    for axis, bit in order:
+        if axis == "sub":
+            offsets = [o for o in offsets if not o & bit]
+        steps.append((axis, bit, offsets))
+    return steps
+
+
+def greet(groups, owners, me):
+    g, s = me
+    barrier = pltpu.get_barrier_semaphore()
+    for r in range(1, groups):
+        pl.semaphore_signal(
+            barrier, inc=1, device_id=(lax.rem(g + r, groups), s), device_id_type=MESH
+        )
+    for r in range(1, owners):
+        pl.semaphore_signal(
+            barrier, inc=1, device_id=(g, lax.rem(s + r, owners)), device_id_type=MESH
+        )
+    pl.semaphore_wait(barrier, groups + owners - 2)
+
+
+def bit_of(index, bit):
+    return lax.rem(lax.div(index, bit), 2)
+
+
+class Halving:
+    def __init__(self, me, steps, rows, first, acc, recv, send_sem, recv_sem):
+        self.me, self.steps, self.first, self.acc = me, steps, first, acc
+        self.recv, self.send_sem, self.recv_sem = recv, send_sem, recv_sem
+        self.copies = {}
+        self.places = []
+        base, x0, nx = 0, 0, rows
+        count = 0
+        g, s = me
+        for axis, bit, offsets in steps:
+            mine = bit_of(g if axis == "grp" else s, bit)
+            flip = bit * (1 - 2 * mine)
+            if axis == "grp":
+                nx = nx // 2
+                aligned = math.gcd(nx, 16)
+                away = pl.multiple_of(x0 + (1 - mine) * nx, aligned)
+                x0 = pl.multiple_of(x0 + mine * nx, aligned)
+                base_away, peer = base, (g + flip, s)
+            else:
+                away, base_away = x0, base + (1 - mine) * bit
+                base, peer = base + mine * bit, (g, s + flip)
+            self.places.append((base, base_away, x0, away, nx, peer, mine, count))
+            count += len(offsets)
+
+    def send(self, k, i):
+        base, base_away, x0, away, nx, peer, mine, count = self.places[k]
+        offset = self.steps[k][2][i]
+        source = self.first if k == 0 else self.acc
+        copy = pltpu.make_async_remote_copy(
+            src_ref=source.at[base_away + offset, :, pl.ds(away, nx)],
+            dst_ref=self.recv[k].at[i],
+            send_sem=self.send_sem.at[count + i],
+            recv_sem=self.recv_sem.at[count + i],
+            device_id=peer,
+            device_id_type=MESH,
+        )
+        copy.start()
+        self.copies[k, i] = copy
+
+    def take(self, k, i):
+        base, base_away, x0, away, nx, peer, mine, count = self.places[k]
+        offset = self.steps[k][2][i]
+        self.copies[k, i].wait_recv()
+        source = self.first if k == 0 else self.acc
+        here = (base + offset, slice(None), pl.ds(x0, nx))
+        self.acc[here] = source[here].astype(jnp.float32) + self.recv[k][i].astype(jnp.float32)
+
+    def send_all(self, k):
+        for i in range(len(self.steps[k][2])):
+            self.send(k, i)
+
+
+def reduce_kernel(
+    groups, owners, steps_f, steps_m, f_ref, j_ref, total_ref, mean_ref, acc_f, acc_m, slab_f, slab_m, *rest
+):
+    count = len(steps_f)
+    recv_f, recv_m = rest[:count], rest[count : 2 * count]
+    f_send, f_recv, m_send, m_recv, g_send, g_recv, h_send, h_recv = rest[2 * count :]
+    me = (lax.axis_index("grp"), lax.axis_index("sub"))
+    g, s = me
+    depth, rows = f_ref.shape[1:3]
+    slab_f[...] = jnp.zeros_like(slab_f)
+    slab_m[...] = jnp.zeros_like(slab_m)
+    greet(groups, owners, me)
+    force = Halving(me, steps_f, rows, f_ref, acc_f, recv_f, f_send, f_recv)
+    image = Halving(me, steps_m, rows, j_ref, acc_m, recv_m, m_send, m_recv)
+    for volume in (force, image):
+        volume.send_all(0)
+    for k in range(count):
+        blocks = [len(v.steps[k][2]) for v in (force, image)]
+        for i in range(max(blocks)):
+            for volume, n in zip((force, image), blocks):
+                if i < n:
+                    volume.take(k, i)
+                    if k + 1 < count and volume.steps[k + 1][0] == "grp":
+                        volume.send(k + 1, i)
+        if k + 1 < count:
+            for volume in (force, image):
+                if volume.steps[k + 1][0] == "sub":
+                    volume.send_all(k + 1)
+    pending = []
+    for n, (volume, slab, edge) in enumerate(((force, slab_f, REACH), (image, slab_m, 1))):
+        base, _, x0, _, nx, _, _, _ = volume.places[-1]
+        place = (pl.ds(edge, depth), pl.ds(x0, nx))
+        slab[place] = volume.acc[base, :, pl.ds(x0, nx)]
+        for r in range(1, groups):
+            peer_g = g + sum(b * (1 - 2 * bit_of(g, b)) for b in bits(groups) if r & b)
+            copy = pltpu.make_async_remote_copy(
+                src_ref=slab.at[place],
+                dst_ref=slab.at[place],
+                send_sem=g_send.at[n * groups + r],
+                recv_sem=g_recv.at[n * groups + r],
+                device_id=(peer_g, s),
+                device_id_type=MESH,
+            )
+            copy.start()
+            pending.append(copy)
+    for copy in pending:
+        copy.wait_recv()
+    halos, at = [], 0
+    for slab, edge in ((slab_f, REACH), (slab_m, 1)):
+        hop, left = 1, edge
+        while left > 0:
+            size = min(left, depth)
+            near = edge - (hop - 1) * depth
+            for up in (True, False):
+                step = hop if up else -hop
+                source = slab.at[pl.ds(edge + depth - size if up else edge, size)]
+                target = slab.at[pl.ds(near - size if up else edge + hop * depth, size)]
+                sends = s + hop < owners if up else s >= hop
+                receives = s >= hop if up else s + hop < owners
+                copy = pltpu.make_async_remote_copy(
+                    src_ref=source,
+                    dst_ref=target,
+                    send_sem=h_send.at[at],
+                    recv_sem=h_recv.at[at],
+                    device_id=(g, lax.rem(s + step + owners, owners)),
+                    device_id_type=MESH,
+                )
+                pl.when(sends)(copy.start)
+                halos.append((copy, sends, receives))
+                at += 1
+            hop, left = hop + 1, left - size
+    for copy, sends, receives in halos:
+        pl.when(receives)(copy.wait_recv)
+    total_ref[...] = slab_f[...]
+    mean_ref[...] = slab_m[...]
+    for copy, sends, receives in halos:
+        pl.when(sends)(copy.wait_send)
+    for copy in pending + list(force.copies.values()) + list(image.copies.values()):
+        copy.wait_send()
+
+
+def reduced(factor, moving):
+    groups, owners = lax.axis_size("grp"), lax.axis_size("sub")
+    depth, rows, lanes = factor.shape
+    slab = depth // owners
+    by_group = [("grp", b) for b in bits(groups)]
+    by_owner = [("sub", b) for b in bits(owners)]
+    order_f = by_group + by_owner
+    order_m = by_group[:1] + by_owner[:1] + by_group[1:] + by_owner[1:]
+    steps_f, steps_m = plan(groups, owners, order_f), plan(groups, owners, order_m)
+    recv = []
+    for n, steps in enumerate((steps_f, steps_m)):
+        nx = rows
+        for k, (axis, _, offsets) in enumerate(steps):
+            nx = nx // 2 if axis == "grp" else nx
+            kind = jnp.bfloat16 if n == 1 and k == 0 else jnp.float32
+            recv.append(pltpu.VMEM((len(offsets), slab, nx, lanes), kind))
+    copies = [sum(len(o) for _, _, o in steps) for steps in (steps_f, steps_m)]
+    halos = 2 * (-(-REACH // slab)) + 2
+    dma = pltpu.SemaphoreType.DMA
+    vmem = pl.BlockSpec(memory_space=pltpu.VMEM)
+    shape_f, shape_m = (slab + 2 * REACH, rows, lanes), (slab + 2, rows, lanes)
+    blocks = (owners, slab, rows, lanes)
+    return pl.pallas_call(
+        functools.partial(reduce_kernel, groups, owners, steps_f, steps_m),
+        out_shape=tuple(jax.ShapeDtypeStruct(x, jnp.float32) for x in (shape_f, shape_m)),
+        in_specs=[vmem] * 2,
+        out_specs=(vmem, vmem),
+        scratch_shapes=[
+            pltpu.VMEM(blocks, jnp.float32),
+            pltpu.VMEM(blocks, jnp.float32),
+            pltpu.VMEM(shape_f, jnp.float32),
+            pltpu.VMEM(shape_m, jnp.float32),
+            *recv,
+            dma((copies[0],)),
+            dma((copies[0],)),
+            dma((copies[1],)),
+            dma((copies[1],)),
+            dma((2 * groups,)),
+            dma((2 * groups,)),
+            dma((halos,)),
+            dma((halos,)),
+        ],
+        compiler_params=pltpu.CompilerParams(
+            collective_id=1, has_side_effects=True, vmem_limit_bytes=56 * 2**20
+        ),
+    )(factor.reshape(blocks), moving.reshape(blocks))
+
+
+def sum_kernel(groups, owners, in_ref, out_ref, row, column, send_sem, recv_sem):
+    me = (lax.axis_index("grp"), lax.axis_index("sub"))
+    g, s = me
+    greet(groups, owners, me)
+    at, copies = 0, []
+    row[0] = in_ref[...]
+    for axis, size, slots in (("grp", groups, row), ("sub", owners, column)):
+        started = []
+        for r in range(1, size):
+            peer = (lax.rem(g + r, size), s) if axis == "grp" else (g, lax.rem(s + r, size))
+            copy = pltpu.make_async_remote_copy(
+                src_ref=slots.at[0],
+                dst_ref=slots.at[r],
+                send_sem=send_sem.at[at],
+                recv_sem=recv_sem.at[at],
+                device_id=peer,
+                device_id_type=MESH,
+            )
+            copy.start()
+            started.append(copy)
+            at += 1
+        for copy in started:
+            copy.wait_recv()
+        copies += started
+        mine = g if axis == "grp" else s
+        total = slots[lax.rem(mine + size, size)]
+        for rank in range(1, size):
+            total = total + slots[lax.rem(mine - rank + size, size)]
+        if axis == "grp":
+            column[0] = total
+        else:
+            out_ref[...] = total
+    for copy in copies:
+        copy.wait_send()
+
+
+def summed(values):
+    groups, owners = lax.axis_size("grp"), lax.axis_size("sub")
+    copies = groups + owners - 2
+    vmem = pl.BlockSpec(memory_space=pltpu.VMEM)
+    shape = (8, 128)
+    rows = jnp.pad(jnp.stack(values), (0, 8 - len(values)))
+    out = pl.pallas_call(
+        functools.partial(sum_kernel, groups, owners),
+        out_shape=jax.ShapeDtypeStruct(shape, jnp.float32),
+        in_specs=[vmem],
+        out_specs=vmem,
+        scratch_shapes=[
+            pltpu.VMEM((groups, *shape), jnp.float32),
+            pltpu.VMEM((owners, *shape), jnp.float32),
+            pltpu.SemaphoreType.DMA((copies,)),
+            pltpu.SemaphoreType.DMA((copies,)),
+        ],
+        compiler_params=pltpu.CompilerParams(collective_id=2, has_side_effects=True),
+    )(jnp.broadcast_to(rows[:, None], shape))
+    return [out[k, 0] for k in range(len(values))]
 
 
 def on_device(template, subjects):
@@ -149,11 +401,11 @@
     slab = template.shape[0]
     subject_count = subjects.shape[0] * lax.axis_size("grp") * lax.axis_size("sub")
     cell_count = depth * height * width
-    mean_image = reduced(subjects[0].astype(jnp.float32)) / subject_count
-    padded_mean = with_halo(mean_image, 1)
     factor, cc = factors(image, subjects[0])
     cc_local = jnp.sum(cc)
-    total = with_halo(reduced(factor), REACH)
+    total, image_sum = reduced(factor, subjects[0])
+    padded_mean = image_sum / subject_count
+    mean_image = padded_mean[1:-1]
 
     reach = REACH + 1
     padded = jnp.pad(image, ((reach, reach), (0, 0), (0, 0)))
@@ -182,9 +434,7 @@
     velocity_square = jnp.sum(mean_velocity * mean_velocity)
     image_square = jnp.sum(mean_image * mean_image)
     groups = lax.axis_size("grp")
-    sums = lax.psum(
-        jnp.stack([cc_local, velocity_square / groups, image_square / groups]), ("grp", "sub")
-    )
+    sums = summed([cc_local, velocity_square / groups, image_square / groups])
     velocity_norm = jnp.sqrt(sums[1] / cell_count + EPSILON)
     image_norm = jnp.sqrt(sums[2] / cell_count + EPSILON)
     velocity = STEP_LENGTH * mean_velocity / velocity_norm

time: 369 us -> 241 us (0.65)
  waiting for transfers between devices: 232 us -> 57.1 us
  Pallas kernels: 32.6 us -> 149 us
  blocking collectives: 54.9 us -> 0 us
  starting transfers between devices: 9.94 us -> 0.04 us
  other arithmetic: 11.4 us -> 7.4 us
    reduce_scatter x4 -> x0, waiting for transfers between devices: 171 us -> none  [the longest x2 126 us: reduced(): part = lax.psum_scatter(part, 'sub', scatter_dimension=0, tiled=True)]
    pallas_call x0 -> x2, Pallas kernels: none -> 116 us  [the longest x1 105 us: reduced(): pl.pallas_call(functools.partial(reduce_kernel, groups, owners, steps_f,...]
    psum x1 -> x0, blocking collectives: 39.5 us -> none  [on_device(): lax.psum(jnp.stack([cc_local, velocity_square / groups, image_square / gr...]
    all_gather x2 -> x0, blocking collectives: 15.4 us -> none  [reduced(): return lax.all_gather(part, 'grp', axis=1, tiled=True)]
    ppermute x4 -> x0, starting transfers between devices: 9.73 us -> none  [the longest x2 7.17 us: with_halo(): before.insert(0, lax.ppermute(slab[length - take:], 'sub', up))]
    ppermute x4 -> x0, waiting for transfers between devices: 7.75 us -> none  [the longest x2 7.74 us: with_halo(): before.insert(0, lax.ppermute(slab[length - take:], 'sub', up))]
    convert_element_type x1 -> x0, other arithmetic: 4.47 us -> none  [on_device(): mean_image = reduced(subjects[0].astype(jnp.float32)) / subject_count]
    all_gather x1, waiting for transfers between devices: 52.1 us -> 56.5 us  [on_device(): image = lax.all_gather(template, 'sub', axis=0, tiled=True)]
  transfers between devices with their start and end apart: 9 -> 1, of which waited for: 5 -> 1; matrix products, arithmetic and copies ran while one was open for 4% -> 0% of each run, Pallas kernels for 9% -> 0%
where the time goes in v2:
time: 241 us; the launch traced here: 240 us
  Pallas kernels  149 us (62%)
  waiting for transfers between devices  57.1 us (24%)
  between operations  18.6 us (8%)
  other arithmetic  7.4 us (3%)
  local copies, waits for them, and re-layouts  4.42 us (2%)
  matrix products  4.11 us (2%)
    pallas_call x1, Pallas kernels, reduced(): pl.pallas_call(functools.partial(reduce_kernel, groups, owners, steps_f,...  105 us
    all_gather x1, waiting for transfers between devices, on_device(): image = lax.all_gather(template, 'sub', axis=0, tiled=True)  56.5 us
    pallas_call x1, Pallas kernels, factors(): pl.pallas_call(factor_kernel, out_shape=(jax.ShapeDtypeStruct((depth, row...  32.6 us
    pallas_call x1, Pallas kernels, summed(): pl.pallas_call(functools.partial(sum_kernel, groups, owners), out_shape=j...  11 us
  transfers between devices with their start and end apart: 1, of which 1 were waited for; matrix products, arithmetic and copies ran while one was open for 0% of the time, Pallas kernels for 0%

profile of v2, /device:TPU:0, one launch (start us, length us, event | category | flops | bytes accessed | tf_op | source)
XLA Modules:
  0.0 240.4 jit_solution(7866440028781112912)
XLA Ops:
  7.2 0.0 all-gather.2.cloned.1.call-start
  7.2 0.7 all-gather.2.cloned.1.call-update
  7.9 0.6 select_convert_fusion.band_ref
  8.5 56.5 %all-gather.2.cloned.1.call-done.i_ref = bf16[96,96,128]{2,1,0:T(8,128)(2,1)} async-done(((bf16[12,96,128]{2,1,0:T(8,128)(2,1)}), bf16[96,96,128]{2,1,0:T(8,128)(2,1)}) %all-gather.2.cloned.1.call-update) | async-done | bytes 2359312 | tf_op jit(solution)/shard_map/all_gather | solution.py:399
  65.0 32.6 %shard_map.49 = (f32[96,96,128]{2,1,0:T(8,128)}, f32[96,128]{1,0:T(8,128)}) custom-call(bf16[96,96,128]{2,1,0:T(8,128)(2,1)} %all-gather.2.cloned.1.call-done.i_ref, bf16[96,96,128]{2,1,0:T(8,128)(2,1)} %bitcast.43, bf16[128,128]{1,0:T(8,128)(2,1)} %select_convert_fusion.band_ref), custom_call_target="tpu_custom_call" | custom-call | flops 2415919104 | bytes 70778880 | tf_op jit(solution)/shard_map/pallas_call | solution.py:112
  97.6 105.2 %shard_map.50 = (f32[22,96,128]{2,1,0:T(8,128)}, f32[14,96,128]{2,1,0:T(8,128)}) custom-call(f32[8,12,96,128]{3,2,1,0:T(8,128)} %bitcast.42, bf16[8,12,96,128]{3,2,1,0:T(8,128)(2,1)} %bitcast.44), custom_call_target="tpu_custom_call" | custom-call | tf_op jit(solution)/shard_map/pallas_call | solution.py:314
  202.8 0.0 copy-start
  202.8 1.3 broadcast_multiply_fusion
  204.1 0.8 fusion.96
  204.8 0.0 copy-done
  204.8 0.0 copy-start.1
  204.8 0.1 fusion.22
  205.0 1.1 copy-done.1
  206.1 0.6 fusion.11
  206.7 0.4 fusion.48
  207.1 0.4 fusion.26
  207.4 0.4 fusion.37
  207.8 1.6 fusion
  209.4 0.0 copy-start.2
  209.4 2.6 %multiply_reduce_fusion = (f32[]{:T(128)}, f32[12,3,128,96]{2,3,1,0:T(8,128)S(1)}) fusion(f32[12,3,96,128]{3,2,1,0:T(8,128)S(1)} %fusion), kind=kOutput, calls=%fused_computation.11 | convolution fusion | flops 511017984 | bytes 3538948 | tf_op jit(solution)/shard_map/ab,zcby->zcay/dot_general | solution.py:430
  213.2 0.0 copy-done.2
  213.3 0.6 reduce_sum.27
  213.9 0.7 select_maximum_fusion
  214.6 0.7 broadcast_in_dim.23.in_ref
  215.3 11.0 %shard_map.51 = f32[8,128]{1,0:T(8,128)} custom-call(f32[8,128]{1,0:T(8,128)} %broadcast_in_dim.23.in_ref), custom_call_target="tpu_custom_call" | custom-call | tf_op jit(solution)/shard_map/pallas_call | solution.py:382
  226.2 1.3 fusion.97
  228.9 0.2 fusion.3
  229.1 1.3 copy.8
  231.1 1.4 fusion.18
Async XLA Ops:
  7.2 57.8 %all-gather.2.cloned.1.call-start = ((), (), s32[]{:S(2)}) async-start(), calls=%async_computation | async-start | bytes 2654208 | tf_op jit(solution)/shard_map/all_gather | solution.py:399
  202.8 2.1 copy-start
  204.8 1.2 copy-start.1
  209.4 3.9 %copy-start.2 = (f32[96,128]{1,0:T(8,128)S(1)}, f32[96,128]{1,0:T(8,128)}, u32[]{:S(2)}) copy-start(f32[96,128]{1,0:T(8,128)} %get-tuple-element.9) | copy-start | bytes 147460
Sparse Core Ops, SparseCore 0:
  10.2 54.7 all-gather.1

commit v3 on v2

--- a/solution.py
+++ b/solution.py
@@ -54,75 +54,66 @@
     return pltpu.roll(nine, rows + 16 - RADIUS, 0)[8 : 8 + rows]
 
 
-def factor_kernel(i_ref, j_ref, band_ref, f_ref, cc_ref, sums):
-    depth, rows, lanes = i_ref.shape
-    chunk = 4
+def row_sums(i_ref, j_ref, band_ref, sums):
+    owners, slab, rows, lanes = i_ref.shape
+    depth = owners * slab
     band = band_ref[...]
     edge = jnp.zeros((RADIUS, rows, lanes), jnp.float32)
     for k in range(5):
         sums[k, :RADIUS] = edge
         sums[k, depth + RADIUS :] = edge
-    cc_ref[...] = jnp.zeros_like(cc_ref)
-
-    @pl.loop(0, depth // chunk)
+
+    @pl.loop(0, owners)
+    def _(block):
+        for z0 in range(0, slab, 3):
+            size = min(3, slab - z0)
+            i16 = i_ref[block, z0 : z0 + size].reshape(size * rows, lanes)
+            j16 = j_ref[block, z0 : z0 + size].reshape(size * rows, lanes)
+            i32, j32 = i16.astype(jnp.float32), j16.astype(jnp.float32)
+            fields = (
+                jnp.dot(i16, band, preferred_element_type=jnp.float32),
+                split_dot(i32 * i32, band),
+                jnp.dot(j16, band, preferred_element_type=jnp.float32),
+                split_dot(j32 * j32, band),
+                split_dot(i32 * j32, band),
+            )
+            for k, field in enumerate(fields):
+                place = pl.ds(block * slab + z0 + RADIUS, size)
+                sums[k, place] = field.reshape(size, rows, lanes)
+
+
+def window_z(a):
+    if len(a) == 4 + 2 * RADIUS:
+        mid = ((a[3] + a[4]) + (a[5] + a[6])) + (a[7] + a[8])
+        p, q = a[1] + a[2], a[9] + a[10]
+        return (mid + (a[0] + p), mid + (p + a[9]), mid + (a[2] + q), mid + (q + a[11]))
+    return [sum(a[c + 1 : c + 2 * RADIUS + 1], a[c]) for c in range(len(a) - 2 * RADIUS)]
+
+
+def block_factors(first, last, i_ref, j_ref, f_ref, cc_ref, sums):
+    slab = i_ref.shape[1]
+    chunk = 4 if slab % 4 == 0 else 1
+    scale = 1.0 / (2 * RADIUS + 1) ** 3
+    parts = slab // chunk
+
+    @pl.loop(first * parts, last * parts)
     def _(step):
-        z = step * chunk
-        i16 = i_ref[pl.ds(z, chunk)].reshape(chunk * rows, lanes)
-        j16 = j_ref[pl.ds(z, chunk)].reshape(chunk * rows, lanes)
-        i32, j32 = i16.astype(jnp.float32), j16.astype(jnp.float32)
-        fields = (
-            jnp.dot(i16, band, preferred_element_type=jnp.float32),
-            split_dot(i32 * i32, band),
-            jnp.dot(j16, band, preferred_element_type=jnp.float32),
-            split_dot(j32 * j32, band),
-            split_dot(i32 * j32, band),
-        )
-        for k, field in enumerate(fields):
-            sums[k, pl.ds(z + RADIUS, chunk)] = field.reshape(chunk, rows, lanes)
-
-    scale = 1.0 / (2 * RADIUS + 1) ** 3
-
-    @pl.loop(0, depth // chunk)
-    def _(step):
-        z = step * chunk
+        block, z0 = lax.div(step, parts), lax.rem(step, parts) * chunk
         planes = []
         for k in range(5):
-            a = [sums[k, z + o] for o in range(chunk + 2 * RADIUS)]
-            mid = ((a[3] + a[4]) + (a[5] + a[6])) + (a[7] + a[8])
-            p, q = a[1] + a[2], a[9] + a[10]
-            outs = (mid + (a[0] + p), mid + (p + a[9]), mid + (a[2] + q), mid + (q + a[11]))
-            planes.append([window_x(o) * scale for o in outs])
+            a = [sums[k, step * chunk + o] for o in range(chunk + 2 * RADIUS)]
+            planes.append([window_x(o) * scale for o in window_z(a)])
         for c in range(chunk):
             mean_i, mean_ii, mean_j, mean_jj, mean_ij = (planes[k][c] for k in range(5))
-            i32 = i_ref[z + c].astype(jnp.float32)
-            j32 = j_ref[z + c].astype(jnp.float32)
+            i32 = i_ref[block, z0 + c].astype(jnp.float32)
+            j32 = j_ref[block, z0 + c].astype(jnp.float32)
             cross = mean_ij - mean_i * mean_j
             var_i = mean_ii - mean_i * mean_i
             var_j = mean_jj - mean_j * mean_j
             ratio = cross / (var_i * var_j + EPSILON)
             slope = cross / (var_i + EPSILON)
-            f_ref[z + c] = 2.0 * ratio * (j32 - mean_j - slope * (i32 - mean_i))
+            f_ref[block, z0 + c] = 2.0 * ratio * (j32 - mean_j - slope * (i32 - mean_i))
             cc_ref[...] += cross * ratio
-
-
-def factors(image, moving):
-    depth, rows, lanes = image.shape
-    cells = depth * rows * lanes
-    vmem = pl.BlockSpec(memory_space=pltpu.VMEM)
-    return pl.pallas_call(
-        factor_kernel,
-        out_shape=(
-            jax.ShapeDtypeStruct((depth, rows, lanes), jnp.float32),
-            jax.ShapeDtypeStruct((rows, lanes), jnp.float32),
-        ),
-        in_specs=[vmem] * 3,
-        out_specs=(vmem, vmem),
-        scratch_shapes=[pltpu.VMEM((5, depth + 2 * RADIUS, rows, lanes), jnp.float32)],
-        compiler_params=pltpu.CompilerParams(vmem_limit_bytes=56 * 2**20),
-        cost_estimate=pl.CostEstimate(
-            flops=cells * lanes * 16, bytes_accessed=cells * 60, transcendentals=2 * cells
-        ),
-    )(image, moving, band_matrix(lanes, RADIUS, False))
 
 
 def bits(size):
@@ -203,39 +194,74 @@
         here = (base + offset, slice(None), pl.ds(x0, nx))
         self.acc[here] = source[here].astype(jnp.float32) + self.recv[k][i].astype(jnp.float32)
 
+    def pass_on(self, k, i):
+        self.take(k, i)
+        if k + 1 < len(self.steps) and self.steps[k + 1][0] == "grp":
+            self.send(k + 1, i)
+
+    def finish(self, k):
+        if k + 1 < len(self.steps) and self.steps[k + 1][0] == "sub":
+            self.send_all(k + 1)
+
+    def advance(self, k):
+        for i in range(len(self.steps[k][2])):
+            self.pass_on(k, i)
+        self.finish(k)
+
     def send_all(self, k):
         for i in range(len(self.steps[k][2])):
             self.send(k, i)
 
 
 def reduce_kernel(
-    groups, owners, steps_f, steps_m, f_ref, j_ref, total_ref, mean_ref, acc_f, acc_m, slab_f, slab_m, *rest
+    groups,
+    owners,
+    steps_f,
+    steps_m,
+    i_ref,
+    j_ref,
+    band_ref,
+    total_ref,
+    mean_ref,
+    cc_ref,
+    sums,
+    acc_f,
+    acc_m,
+    slab_f,
+    slab_m,
+    *rest,
 ):
     count = len(steps_f)
     recv_f, recv_m = rest[:count], rest[count : 2 * count]
     f_send, f_recv, m_send, m_recv, g_send, g_recv, h_send, h_recv = rest[2 * count :]
     me = (lax.axis_index("grp"), lax.axis_index("sub"))
     g, s = me
-    depth, rows = f_ref.shape[1:3]
+    depth, rows = j_ref.shape[1:3]
     slab_f[...] = jnp.zeros_like(slab_f)
     slab_m[...] = jnp.zeros_like(slab_m)
     greet(groups, owners, me)
-    force = Halving(me, steps_f, rows, f_ref, acc_f, recv_f, f_send, f_recv)
+    force = Halving(me, steps_f, rows, acc_f, acc_f, recv_f, f_send, f_recv)
     image = Halving(me, steps_m, rows, j_ref, acc_m, recv_m, m_send, m_recv)
-    for volume in (force, image):
-        volume.send_all(0)
-    for k in range(count):
-        blocks = [len(v.steps[k][2]) for v in (force, image)]
-        for i in range(max(blocks)):
-            for volume, n in zip((force, image), blocks):
-                if i < n:
-                    volume.take(k, i)
-                    if k + 1 < count and volume.steps[k + 1][0] == "grp":
-                        volume.send(k + 1, i)
-        if k + 1 < count:
-            for volume in (force, image):
-                if volume.steps[k + 1][0] == "sub":
-                    volume.send_all(k + 1)
+    image.send_all(0)
+    cc_ref[...] = jnp.zeros_like(cc_ref)
+    row_sums(i_ref, j_ref, band_ref, sums)
+    image.advance(0)
+    lead = [owners * k // (count - 1) for k in range(count)]
+    waiting = []
+    for k in range(1, count):
+        first, last = lead[k - 1], lead[k]
+        block_factors(first, last, i_ref, j_ref, acc_f, cc_ref, sums)
+        for i in range(first, last):
+            force.send(0, i)
+        image.advance(k)
+        for i in waiting:
+            force.pass_on(0, i)
+        waiting = range(first, last)
+    for i in waiting:
+        force.pass_on(0, i)
+    force.finish(0)
+    for k in range(1, count):
+        force.advance(k)
     pending = []
     for n, (volume, slab, edge) in enumerate(((force, slab_f, REACH), (image, slab_m, 1))):
         base, _, x0, _, nx, _, _, _ = volume.places[-1]
@@ -289,9 +315,9 @@
         copy.wait_send()
 
 
-def reduced(factor, moving):
+def reduced(image, moving):
     groups, owners = lax.axis_size("grp"), lax.axis_size("sub")
-    depth, rows, lanes = factor.shape
+    depth, rows, lanes = moving.shape
     slab = depth // owners
     by_group = [("grp", b) for b in bits(groups)]
     by_owner = [("sub", b) for b in bits(owners)]
@@ -313,10 +339,13 @@
     blocks = (owners, slab, rows, lanes)
     return pl.pallas_call(
         functools.partial(reduce_kernel, groups, owners, steps_f, steps_m),
-        out_shape=tuple(jax.ShapeDtypeStruct(x, jnp.float32) for x in (shape_f, shape_m)),
-        in_specs=[vmem] * 2,
-        out_specs=(vmem, vmem),
+        out_shape=tuple(
+            jax.ShapeDtypeStruct(x, jnp.float32) for x in (shape_f, shape_m, (rows, lanes))
+        ),
+        in_specs=[vmem] * 3,
+        out_specs=(vmem,) * 3,
         scratch_shapes=[
+            pltpu.VMEM((5, depth + 2 * RADIUS, rows, lanes), jnp.float32),
             pltpu.VMEM(blocks, jnp.float32),
             pltpu.VMEM(blocks, jnp.float32),
             pltpu.VMEM(shape_f, jnp.float32),
@@ -332,9 +361,9 @@
             dma((halos,)),
         ],
         compiler_params=pltpu.CompilerParams(
-            collective_id=1, has_side_effects=True, vmem_limit_bytes=56 * 2**20
+            collective_id=1, has_side_effects=True, vmem_limit_bytes=60 * 2**20
         ),
-    )(factor.reshape(blocks), moving.reshape(blocks))
+    )(image.reshape(blocks), moving.reshape(blocks), band_matrix(lanes, RADIUS, False))
 
 
 def sum_kernel(groups, owners, in_ref, out_ref, row, column, send_sem, recv_sem):
@@ -395,15 +424,78 @@
     return [out[k, 0] for k in range(len(values))]
 
 
+def gather_kernel(groups, owners, t_ref, out_ref, whole, send_sem, recv_sem):
+    me = (lax.axis_index("grp"), lax.axis_index("sub"))
+    g, s = me
+    half = t_ref.shape[1] // 2
+    core = bit_of(g, 1)
+    whole[s] = t_ref[...]
+    greet(groups, owners, me)
+    x0 = pl.multiple_of(core * half, math.gcd(half, 16))
+    at, copies, across = 0, [], []
+
+    def start(block, peer):
+        nonlocal at
+        place = whole.at[block, :, pl.ds(x0, half)]
+        copy = pltpu.make_async_remote_copy(
+            src_ref=place,
+            dst_ref=place,
+            send_sem=send_sem.at[at],
+            recv_sem=recv_sem.at[at],
+            device_id=peer,
+            device_id_type=MESH,
+        )
+        copy.start()
+        copies.append(copy)
+        at += 1
+        return copy
+
+    def flipped(pattern):
+        return s + sum(b * (1 - 2 * bit_of(s, b)) for b in bits(owners) if pattern & b)
+
+    held = [0]
+    for bit in reversed(bits(owners)):
+        started = [start(flipped(p), (g, flipped(bit))) for p in held]
+        for p, copy in zip(held, started):
+            copy.wait_recv()
+            across.append(start(flipped(p | bit), (g + 1 - 2 * core, s)))
+        held = held + [p | bit for p in held]
+    for copy in across:
+        copy.wait_recv()
+    out_ref[...] = whole[...]
+    for copy in copies:
+        copy.wait_send()
+
+
+def gathered(template):
+    groups, owners = lax.axis_size("grp"), lax.axis_size("sub")
+    vmem = pl.BlockSpec(memory_space=pltpu.VMEM)
+    shape = (owners, *template.shape)
+    copies = 2 * (owners - 1)
+    return pl.pallas_call(
+        functools.partial(gather_kernel, groups, owners),
+        out_shape=jax.ShapeDtypeStruct(shape, template.dtype),
+        in_specs=[vmem],
+        out_specs=vmem,
+        scratch_shapes=[
+            pltpu.VMEM(shape, template.dtype),
+            pltpu.SemaphoreType.DMA((copies,)),
+            pltpu.SemaphoreType.DMA((copies,)),
+        ],
+        compiler_params=pltpu.CompilerParams(
+            collective_id=3, has_side_effects=True, vmem_limit_bytes=32 * 2**20
+        ),
+    )(template).reshape(-1, *template.shape[1:])
+
+
 def on_device(template, subjects):
-    image = lax.all_gather(template, "sub", axis=0, tiled=True)
+    image = gathered(template)
     depth, height, width = image.shape
     slab = template.shape[0]
     subject_count = subjects.shape[0] * lax.axis_size("grp") * lax.axis_size("sub")
     cell_count = depth * height * width
-    factor, cc = factors(image, subjects[0])
+    total, image_sum, cc = reduced(image, subjects[0])
     cc_local = jnp.sum(cc)
-    total, image_sum = reduced(factor, subjects[0])
     padded_mean = image_sum / subject_count
     mean_image = padded_mean[1:-1]
 

time: 241 us -> 197 us (0.82)
  waiting for transfers between devices: 57.1 us -> 0 us
  Pallas kernels: 149 us -> 174 us
  between operations: 18.6 us -> 5.23 us
    all_gather x1 -> x0, waiting for transfers between devices: 56.5 us -> none  [on_device(): image = lax.all_gather(template, 'sub', axis=0, tiled=True)]
    pallas_call x1, Pallas kernels: 105 us -> 124 us  [reduced(): pl.pallas_call(functools.partial(reduce_kernel, groups, owners, steps_f,...]
    pallas_call x1, Pallas kernels: 11 us -> 13.9 us  [summed(): pl.pallas_call(functools.partial(sum_kernel, groups, owners), out_shape=j...]
    pallas_call x1, Pallas kernels: 32.6 us -> 35.5 us  [gathered(): pl.pallas_call(functools.partial(gather_kernel, groups, owners), out_shap...]
  transfers between devices with their start and end apart: 1 -> 0, of which waited for: 1 -> 0; matrix products, arithmetic and copies ran while one was open for 0% -> 0% of each run, Pallas kernels for 0% -> 0%
where the time goes in v3:
time: 197 us; the launch traced here: 196 us
  Pallas kernels  174 us (88%)
  other arithmetic  7.4 us (4%)
  local copies, waits for them, and re-layouts  5.53 us (3%)
  between operations  5.23 us (3%)
  matrix products  4.11 us (2%)
    pallas_call x1, Pallas kernels, reduced(): pl.pallas_call(functools.partial(reduce_kernel, groups, owners, steps_f,...  124 us
    pallas_call x1, Pallas kernels, gathered(): pl.pallas_call(functools.partial(gather_kernel, groups, owners), out_shap...  35.5 us
    pallas_call x1, Pallas kernels, summed(): pl.pallas_call(functools.partial(sum_kernel, groups, owners), out_shape=j...  13.9 us

profile of v3, /device:TPU:0, one launch (start us, length us, event | category | flops | bytes accessed | tf_op | source)
XLA Modules:
  0.0 196.2 jit_solution(9553287624792335176)
XLA Ops:
  0.6 0.0 copy-start.1
  0.6 1.0 copy-done.1
  1.6 35.5 %shard_map.49.i_ref = bf16[8,12,96,128]{3,2,1,0:T(8,128)(2,1)S(1)} custom-call(bf16[12,96,128]{2,1,0:T(8,128)(2,1)S(1)} %copy-done.1), custom_call_target="tpu_custom_call" | custom-call | tf_op jit(solution)/shard_map/pallas_call | solution.py:475
  37.1 0.0 copy-start
  37.1 0.1 fusion.22
  37.2 1.3 copy-done
  38.5 0.6 select_convert_fusion.band_ref
  39.1 124.5 %shard_map.50 = (f32[22,96,128]{2,1,0:T(8,128)}, f32[14,96,128]{2,1,0:T(8,128)}, f32[96,128]{1,0:T(8,128)}) custom-call(bf16[8,12,96,128]{3,2,1,0:T(8,128)(2,1)} %copy-done, bf16[8,12,96,128]{3,2,1,0:T(8,128)(2,1)} %bitcast.42, bf16[128,128]{1,0:T(8,128)(2,1)} %select_convert_fusion.band_ref), custom_call_target="tpu_custom_call" | custom-call | tf_op jit(solution)/shard_map/pallas_call | solution.py:340
  163.6 1.9 fusion.11
  165.5 0.4 fusion.26
  165.9 0.4 fusion.37
  166.2 0.4 fusion.48
  166.6 1.6 fusion
  168.2 0.0 copy-start.2
  168.2 2.6 %multiply_reduce_fusion = (f32[]{:T(128)}, f32[12,3,128,96]{2,3,1,0:T(8,128)S(1)}) fusion(f32[12,3,96,128]{3,2,1,0:T(8,128)S(1)} %fusion), kind=kOutput, calls=%fused_computation.11 | convolution fusion | flops 511017984 | bytes 3538948 | tf_op jit(solution)/shard_map/ab,zcby->zcay/dot_general | solution.py:522
  170.7 0.0 copy-start.3
  171.4 0.0 copy-done.2
  171.4 0.1 broadcast_multiply_fusion
  171.5 0.8 fusion.96
  172.9 0.0 copy-done.3
  172.9 0.6 reduce_sum.27
  173.5 0.7 select_maximum_fusion
  174.2 0.7 broadcast_in_dim.23.in_ref
  174.9 13.9 %shard_map.51 = f32[8,128]{1,0:T(8,128)} custom-call(f32[8,128]{1,0:T(8,128)} %broadcast_in_dim.23.in_ref), custom_call_target="tpu_custom_call" | custom-call | tf_op jit(solution)/shard_map/pallas_call | solution.py:411
  188.8 1.3 fusion.97
  190.8 0.2 fusion.3
  191.7 1.4 fusion.18
  193.1 1.3 copy.6
Async XLA Ops:
  0.6 1.0 copy-start.1
  37.1 1.4 copy-start
  168.2 3.2 %copy-start.2 = (f32[14,96,128]{2,1,0:T(8,128)S(1)}, f32[14,96,128]{2,1,0:T(8,128)}, u32[]{:S(2)}) copy-start(f32[14,96,128]{2,1,0:T(8,128)} %get-tuple-element.8) | copy-start | bytes 2064388
  170.7 2.1 %copy-start.3 = (f32[96,128]{1,0:T(8,128)S(1)}, f32[96,128]{1,0:T(8,128)}, u32[]{:S(2)}) copy-start(f32[96,128]{1,0:T(8,128)} %get-tuple-element.7) | copy-start | bytes 147460

commit v4 on v3

--- a/solution.py
+++ b/solution.py
@@ -253,7 +253,6 @@
         block_factors(first, last, i_ref, j_ref, acc_f, cc_ref, sums)
         for i in range(first, last):
             force.send(0, i)
-        image.advance(k)
         for i in waiting:
             force.pass_on(0, i)
         waiting = range(first, last)
@@ -261,7 +260,10 @@
         force.pass_on(0, i)
     force.finish(0)
     for k in range(1, count):
-        force.advance(k)
+        image.advance(k)
+        if k > 1:
+            force.advance(k - 1)
+    force.advance(count - 1)
     pending = []
     for n, (volume, slab, edge) in enumerate(((force, slab_f, REACH), (image, slab_m, 1))):
         base, _, x0, _, nx, _, _, _ = volume.places[-1]
@@ -322,7 +324,7 @@
     by_group = [("grp", b) for b in bits(groups)]
     by_owner = [("sub", b) for b in bits(owners)]
     order_f = by_group + by_owner
-    order_m = by_group[:1] + by_owner[:1] + by_group[1:] + by_owner[1:]
+    order_m = by_group[:1] + by_owner + by_group[1:]
     steps_f, steps_m = plan(groups, owners, order_f), plan(groups, owners, order_m)
     recv = []
     for n, steps in enumerate((steps_f, steps_m)):

time: 197 us -> 178 us (0.904)
  Pallas kernels: 174 us -> 155 us
    pallas_call x1, Pallas kernels: 124 us -> 109 us  [reduced(): pl.pallas_call(functools.partial(reduce_kernel, groups, owners, steps_f,...]
    pallas_call x1, Pallas kernels: 13.9 us -> 11 us  [summed(): pl.pallas_call(functools.partial(sum_kernel, groups, owners), out_shape=j...]
where the time goes in v4:
time: 178 us
  Pallas kernels  155 us (87%)
  other arithmetic  7.4 us (4%)
  local copies, waits for them, and re-layouts  5.53 us (3%)
  between operations  5.23 us (3%)
  matrix products  4.11 us (2%)
    pallas_call x1, Pallas kernels, reduced(): pl.pallas_call(functools.partial(reduce_kernel, groups, owners, steps_f,...  109 us
    pallas_call x1, Pallas kernels, gathered(): pl.pallas_call(functools.partial(gather_kernel, groups, owners), out_shap...  35.5 us
    pallas_call x1, Pallas kernels, summed(): pl.pallas_call(functools.partial(sum_kernel, groups, owners), out_shape=j...  11 us

profile of v4, /device:TPU:0, one launch (start us, length us, event | category | flops | bytes accessed | tf_op | source)
XLA Modules:
  0.0 177.5 jit_solution(5393652525134625045)
XLA Ops:
  0.6 0.0 copy-start.1
  0.6 1.0 copy-done.1
  1.6 35.5 %shard_map.49.i_ref = bf16[8,12,96,128]{3,2,1,0:T(8,128)(2,1)S(1)} custom-call(bf16[12,96,128]{2,1,0:T(8,128)(2,1)S(1)} %copy-done.1), custom_call_target="tpu_custom_call" | custom-call | tf_op jit(solution)/shard_map/pallas_call | solution.py:477
  37.1 0.0 copy-start
  37.1 0.1 fusion.22
  37.2 1.3 copy-done
  38.5 0.6 select_convert_fusion.band_ref
  39.1 108.8 %shard_map.50 = (f32[22,96,128]{2,1,0:T(8,128)}, f32[14,96,128]{2,1,0:T(8,128)}, f32[96,128]{1,0:T(8,128)}) custom-call(bf16[8,12,96,128]{3,2,1,0:T(8,128)(2,1)} %copy-done, bf16[8,12,96,128]{3,2,1,0:T(8,128)(2,1)} %bitcast.42, bf16[128,128]{1,0:T(8,128)(2,1)} %select_convert_fusion.band_ref), custom_call_target="tpu_custom_call" | custom-call | tf_op jit(solution)/shard_map/pallas_call | solution.py:342
  148.0 1.9 %fusion.11 = (f32[22,96,128]{2,1,0:T(8,128)S(1)}, f32[22,96,128]{2,1,0:T(8,128)S(1)}, f32[22,96,128]{2,1,0:T(8,128)S(1)}) fusion(f32[22,96,128]{2,1,0:T(8,128)} %get-tuple-element.6, f32[24,96,128]{2,1,0:T(8,128)S(1)} %fusion.22), kind=kLoop, calls=%fused_computation.22 | loop fusion | flops 2433024 | bytes 7667712 | tf_op jit(solution)/shard_map/mul | solution.py:516
  149.8 0.4 fusion.26
  150.2 0.4 fusion.37
  150.6 0.4 fusion.48
  150.9 1.6 fusion
  152.5 0.0 copy-start.2
  152.5 2.6 %multiply_reduce_fusion = (f32[]{:T(128)}, f32[12,3,128,96]{2,3,1,0:T(8,128)S(1)}) fusion(f32[12,3,96,128]{3,2,1,0:T(8,128)S(1)} %fusion), kind=kOutput, calls=%fused_computation.11 | convolution fusion | flops 511017984 | bytes 3538948 | tf_op jit(solution)/shard_map/ab,zcby->zcay/dot_general | solution.py:524
  155.1 0.0 copy-start.3
  155.7 0.0 copy-done.2
  155.8 0.1 broadcast_multiply_fusion
  155.8 0.8 fusion.96
  157.2 0.0 copy-done.3
  157.2 0.6 reduce_sum.27
  157.8 0.7 select_maximum_fusion
  158.6 0.7 broadcast_in_dim.23.in_ref
  159.2 11.0 %shard_map.51 = f32[8,128]{1,0:T(8,128)} custom-call(f32[8,128]{1,0:T(8,128)} %broadcast_in_dim.23.in_ref), custom_call_target="tpu_custom_call" | custom-call | tf_op jit(solution)/shard_map/pallas_call | solution.py:413
  170.2 1.3 fusion.97
  172.2 0.2 fusion.3
  173.1 1.4 fusion.18
  174.4 1.3 copy.6
Async XLA Ops:
  0.6 1.0 copy-start.1
  37.1 1.4 copy-start
  152.5 3.2 %copy-start.2 = (f32[14,96,128]{2,1,0:T(8,128)S(1)}, f32[14,96,128]{2,1,0:T(8,128)}, u32[]{:S(2)}) copy-start(f32[14,96,128]{2,1,0:T(8,128)} %get-tuple-element.8) | copy-start | bytes 2064388
  155.1 2.1 %copy-start.3 = (f32[96,128]{1,0:T(8,128)S(1)}, f32[96,128]{1,0:T(8,128)}, u32[]{:S(2)}) copy-start(f32[96,128]{1,0:T(8,128)} %get-tuple-element.7) | copy-start | bytes 147460

commit v5 on v4

--- a/solution.py
+++ b/solution.py
@@ -263,9 +263,10 @@
         image.advance(k)
         if k > 1:
             force.advance(k - 1)
-    force.advance(count - 1)
     pending = []
-    for n, (volume, slab, edge) in enumerate(((force, slab_f, REACH), (image, slab_m, 1))):
+    for n, (volume, slab, edge) in enumerate(((image, slab_m, 1), (force, slab_f, REACH))):
+        if n == 1:
+            force.advance(count - 1)
         base, _, x0, _, nx, _, _, _ = volume.places[-1]
         place = (pl.ds(edge, depth), pl.ds(x0, nx))
         slab[place] = volume.acc[base, :, pl.ds(x0, nx)]

time: 178 us -> 174 us (0.978)
  Pallas kernels: 155 us -> 151 us
    pallas_call x1, Pallas kernels: 109 us -> 105 us  [reduced(): pl.pallas_call(functools.partial(reduce_kernel, groups, owners, steps_f,...]
where the time goes in v5:
time: 174 us
  Pallas kernels  151 us (87%)
  other arithmetic  7.4 us (4%)
  local copies, waits for them, and re-layouts  5.53 us (3%)
  between operations  5.23 us (3%)
  matrix products  4.12 us (2%)
    pallas_call x1, Pallas kernels, reduced(): pl.pallas_call(functools.partial(reduce_kernel, groups, owners, steps_f,...  105 us
    pallas_call x1, Pallas kernels, gathered(): pl.pallas_call(functools.partial(gather_kernel, groups, owners), out_shap...  35.5 us
    pallas_call x1, Pallas kernels, summed(): pl.pallas_call(functools.partial(sum_kernel, groups, owners), out_shape=j...  10.3 us
    unnamed x9, local copies, waits for them, and re-layouts  3.56 us

profile of v5, /device:TPU:0, one launch (start us, length us, event | category | flops | bytes accessed | tf_op | source)
XLA Modules:
  0.0 173.5 jit_solution(11720544022999097278)
XLA Ops:
  0.6 0.0 copy-start.1
  0.6 1.0 copy-done.1
  1.6 35.5 %shard_map.49.i_ref = bf16[8,12,96,128]{3,2,1,0:T(8,128)(2,1)S(1)} custom-call(bf16[12,96,128]{2,1,0:T(8,128)(2,1)S(1)} %copy-done.1), custom_call_target="tpu_custom_call" | custom-call | tf_op jit(solution)/shard_map/pallas_call | solution.py:478
  37.1 0.0 copy-start
  37.1 0.1 fusion.22
  37.2 1.3 copy-done
  38.5 0.6 select_convert_fusion.band_ref
  39.1 105.5 %shard_map.50 = (f32[22,96,128]{2,1,0:T(8,128)}, f32[14,96,128]{2,1,0:T(8,128)}, f32[96,128]{1,0:T(8,128)}) custom-call(bf16[8,12,96,128]{3,2,1,0:T(8,128)(2,1)} %copy-done, bf16[8,12,96,128]{3,2,1,0:T(8,128)(2,1)} %bitcast.42, bf16[128,128]{1,0:T(8,128)(2,1)} %select_convert_fusion.band_ref), custom_call_target="tpu_custom_call" | custom-call | tf_op jit(solution)/shard_map/pallas_call | solution.py:343
  144.6 1.9 %fusion.11 = (f32[22,96,128]{2,1,0:T(8,128)S(1)}, f32[22,96,128]{2,1,0:T(8,128)S(1)}, f32[22,96,128]{2,1,0:T(8,128)S(1)}) fusion(f32[22,96,128]{2,1,0:T(8,128)} %get-tuple-element.6, f32[24,96,128]{2,1,0:T(8,128)S(1)} %fusion.22), kind=kLoop, calls=%fused_computation.22 | loop fusion | flops 2433024 | bytes 7667712 | tf_op jit(solution)/shard_map/mul | solution.py:517
  146.5 0.4 fusion.26
  146.8 0.4 fusion.37
  147.2 0.4 fusion.48
  147.6 1.6 fusion
  149.2 0.0 copy-start.2
  149.2 2.6 %multiply_reduce_fusion = (f32[]{:T(128)}, f32[12,3,128,96]{2,3,1,0:T(8,128)S(1)}) fusion(f32[12,3,96,128]{3,2,1,0:T(8,128)S(1)} %fusion), kind=kOutput, calls=%fused_computation.11 | convolution fusion | flops 511017984 | bytes 3538948 | tf_op jit(solution)/shard_map/ab,zcby->zcay/dot_general | solution.py:525
  151.7 0.0 copy-start.3
  152.4 0.0 copy-done.2
  152.4 0.1 broadcast_multiply_fusion
  152.5 0.8 fusion.96
  153.9 0.0 copy-done.3
  153.9 0.6 reduce_sum.27
  154.5 0.7 select_maximum_fusion
  155.2 0.7 broadcast_in_dim.23.in_ref
  155.9 10.3 %shard_map.51 = f32[8,128]{1,0:T(8,128)} custom-call(f32[8,128]{1,0:T(8,128)} %broadcast_in_dim.23.in_ref), custom_call_target="tpu_custom_call" | custom-call | tf_op jit(solution)/shard_map/pallas_call | solution.py:414
  166.2 1.3 fusion.97
  168.2 0.2 fusion.3
  169.1 1.4 fusion.18
  170.4 1.3 copy.6
Async XLA Ops:
  0.6 1.0 copy-start.1
  37.1 1.4 copy-start
  149.2 3.2 %copy-start.2 = (f32[14,96,128]{2,1,0:T(8,128)S(1)}, f32[14,96,128]{2,1,0:T(8,128)}, u32[]{:S(2)}) copy-start(f32[14,96,128]{2,1,0:T(8,128)} %get-tuple-element.8) | copy-start | bytes 2064388
  151.7 2.1 %copy-start.3 = (f32[96,128]{1,0:T(8,128)S(1)}, f32[96,128]{1,0:T(8,128)}, u32[]{:S(2)}) copy-start(f32[96,128]{1,0:T(8,128)} %get-tuple-element.7) | copy-start | bytes 147460
